TPU v7x, 32 devices: a whole 2x2x4 slice. The times are simulated.
32 devices in a mesh: rep: 2 (over y), head: 16 (over z, x, core).
Axes of the slice: x: 2, y: 2, z: 4, core: 2. Of those that a mesh axis runs over, the one named last changes fastest.
Arguments:
- query: bfloat16 [2, 2048, 8192], P('rep', 'head'), may hold values from -16 to 16
- key: bfloat16 [2, 2048, 1024], P('rep', 'head'), may hold values from -16 to 16
- value: bfloat16 [2, 2048, 1024], P('rep', 'head'), may hold values from -6 to 6
- lengths: int32 [2, 8], P('rep'), may hold values from 1 to 1024, 2048 in all within a row
Outputs:
- attended: bfloat16 [2, 2048, 8192], P('rep', 'head')
Inputs may be any that keep to these rules, and one draw needn't show every extreme that they name: Each slab's 8 lengths sum to 2048, and the longest is exactly 1024.
All inputs are finite; a program needn't handle non-finite values.
Results may differ from a plain program's by a relative error of at most 0.0038.
Values may be sent and summed in bfloat16 or wider, within the bound.
No kernel may reach another device: no remote copies, remote signals or barrier semaphores. Data moves between devices by JAX's collectives and lax.ppermute only.
A program may use at most 64 MiB of HBM per device.

v0:
```python
import jax
import jax.numpy as jnp
from jax import lax
from jax.sharding import PartitionSpec as P

Q_HEADS = 64
KV_HEADS = 8
HEAD_DIM = 128


def doc_starts(doc_lengths, count):
    ends = jnp.cumsum(doc_lengths)
    places = jnp.arange(count, dtype=jnp.int32)
    picked = jnp.where(ends[None, :] <= places[:, None], doc_lengths[None, :], 0)
    return jnp.sum(picked, axis=1)


def attend_tile(queries, keys, values, starts, index, tile, offset):
    heads = queries.shape[1]
    q_block = lax.dynamic_slice_in_dim(queries, (index - offset) * tile, tile, 0)
    q_pos = index * tile + jnp.arange(tile, dtype=jnp.int32)
    q_start = lax.dynamic_slice_in_dim(starts, index * tile, tile, 0)
    first = q_start[0] // tile
    scale = float(HEAD_DIM) ** (-0.5)

    def visit(block, carry):
        top, total, accum = carry
        k_block = lax.dynamic_slice_in_dim(keys, (block - offset) * tile, tile, 0)
        v_block = lax.dynamic_slice_in_dim(values, (block - offset) * tile, tile, 0)
        scores = (
            jnp.einsum("qhd,khd->hqk", q_block, k_block, preferred_element_type=jnp.float32) * scale
        )
        k_pos = block * tile + jnp.arange(tile, dtype=jnp.int32)
        allowed = (k_pos[None, :] <= q_pos[:, None]) & (k_pos[None, :] >= q_start[:, None])
        scores = jnp.where(allowed[None], scores, jnp.float32(-1e30))
        new_top = jnp.maximum(top, jnp.max(scores, axis=2))
        weights = jnp.where(allowed[None], jnp.exp(scores - new_top[:, :, None]), jnp.float32(0.0))
        factor = jnp.exp(top - new_top)
        product = jnp.einsum(
            "hqk,khd->hqd",
            weights.astype(jnp.bfloat16),
            v_block,
            preferred_element_type=jnp.float32,
        )
        accum = accum * factor[:, :, None] + product
        total = total * factor + jnp.sum(weights, axis=2)
        return (new_top, total, accum)

    start_state = (
        jnp.full((heads, tile), -1e30, jnp.float32),
        jnp.zeros((heads, tile), jnp.float32),
        jnp.zeros((heads, tile, HEAD_DIM), jnp.float32),
    )
    top, total, accum = lax.fori_loop(first, (index + 1).astype(jnp.int32), visit, start_state)
    result = (accum / total[:, :, None]).astype(jnp.bfloat16)
    return jnp.transpose(result, (1, 0, 2))


def attend_range(queries, keys, values, starts, lower, upper, tile, offset):
    blank = jnp.zeros(queries.shape, jnp.bfloat16)

    def place(index, filled):
        block = attend_tile(queries, keys, values, starts, index, tile, offset)
        return lax.dynamic_update_slice_in_dim(filled, block, (index - offset) * tile, 0)

    return lax.fori_loop(lower, upper, place, blank)


def local(query, key, value, lengths):
    tok_rows = query.shape[1]
    devices = lax.axis_size("head")
    count = tok_rows * devices
    tile = min(512, count)
    ntiles = count // tile
    group = Q_HEADS // KV_HEADS
    q_heads = query.reshape(tok_rows, Q_HEADS, HEAD_DIM)
    k_heads = jnp.repeat(key.reshape(tok_rows, KV_HEADS, HEAD_DIM), group, axis=1)
    v_heads = jnp.repeat(value.reshape(tok_rows, KV_HEADS, HEAD_DIM), group, axis=1)
    queries, keys, values = (
        lax.all_to_all(q_heads, "head", split_axis=1, concat_axis=0, tiled=True),
        lax.all_to_all(k_heads, "head", split_axis=1, concat_axis=0, tiled=True),
        lax.all_to_all(v_heads, "head", split_axis=1, concat_axis=0, tiled=True),
    )
    doc_lengths = lengths[0]
    starts = doc_starts(doc_lengths, count)
    outputs = attend_range(queries, keys, values, starts, jnp.int32(0), jnp.int32(ntiles), tile, 0)
    back = lax.all_to_all(outputs, "head", split_axis=0, concat_axis=1, tiled=True)
    return back.reshape(1, tok_rows, Q_HEADS * HEAD_DIM)


def solution(mesh):
    placed = (
        P("rep", "head", None),
        P("rep", "head", None),
        P("rep", "head", None),
        P("rep", None),
    )
    return jax.shard_map(
        local, mesh=mesh, in_specs=placed, out_specs=P("rep", "head", None), check_vma=False
    )
```

profile of v0, /device:TPU:17, one launch (start us, length us, event | category | flops | bytes accessed | tf_op | source)
XLA Modules:
  0.0 308.3 jit_solution(3913730356097677892)
XLA Ops:
  2.9 6.5 %all-to-all-start.1 = ((bf16[128,64,128]{2,0,1:T(8,128)(2,1)}), bf16[128,64,128]{2,0,1:T(8,128)(2,1)S(1)}, u32[]{:S(2)}, u32[]{:S(2)}) async-start(bf16[128,64,128]{2,0,1:T(8,128)(2,1)} %bitcast.60), calls=%async_computation.1 | async-start | bytes 4194304 | tf_op jit(solution)/shard_map/all_to_all | solution.py:81
  9.5 47.0 %all-to-all-done.1 = bf16[128,64,128]{2,0,1:T(8,128)(2,1)S(1)} async-done(((bf16[128,64,128]{2,0,1:T(8,128)(2,1)}), bf16[128,64,128]{2,0,1:T(8,128)(2,1)S(1)}, u32[]{:S(2)}, u32[]{:S(2)}) %all-to-all-start.1) | async-done | bytes 2097184 | tf_op jit(solution)/shard_map/all_to_all | solution.py:81
  58.5 5.2 %all-to-all-start.2 = ((bf16[128,64,128]{2,0,1:T(8,128)(2,1)}), bf16[128,64,128]{2,0,1:T(8,128)(2,1)}, u32[]{:S(2)}, u32[]{:S(2)}) async-start(bf16[128,64,128]{2,0,1:T(8,128)(2,1)} %bitcast.61), calls=%async_computation.2 | async-start | bytes 4194304 | tf_op jit(solution)/shard_map/all_to_all | solution.py:82
  63.7 4.1 %copy.31 = bf16[1,128,8192]{1,2,0:T(8,128)(2,1)} copy(bf16[1,128,8192]{2,1,0:T(8,128)(2,1)} %param.8) | data formatting | bytes 4194304 | tf_op args[0]
  67.7 43.2 %all-to-all-done.2 = bf16[128,64,128]{2,0,1:T(8,128)(2,1)} async-done(((bf16[128,64,128]{2,0,1:T(8,128)(2,1)}), bf16[128,64,128]{2,0,1:T(8,128)(2,1)}, u32[]{:S(2)}, u32[]{:S(2)}) %all-to-all-start.2) | async-done | bytes 2097184 | tf_op jit(solution)/shard_map/all_to_all | solution.py:82
  110.9 5.2 %all-to-all-start = ((bf16[128,64,128]{0,2,1:T(8,128)(2,1)}), bf16[128,64,128]{0,2,1:T(8,128)(2,1)}, u32[]{:S(2)}, u32[]{:S(2)}) async-start(bf16[128,64,128]{0,2,1:T(8,128)(2,1)} %bitcast.59), calls=%async_computation | async-start | bytes 4194304 | tf_op jit(solution)/shard_map/all_to_all | solution.py:80
  118.2 3.2 %copy.37 = bf16[16,128,4,128]{3,1,0,2:T(8,128)(2,1)} copy(bf16[16,128,4,128]{3,1,2,0:T(8,128)(2,1)} %bitcast.16) | data formatting | bytes 4194304 | tf_op jit(solution)/shard_map/all_to_all | solution.py:82
  121.4 41.9 %all-to-all-done = bf16[128,64,128]{0,2,1:T(8,128)(2,1)} async-done(((bf16[128,64,128]{0,2,1:T(8,128)(2,1)}), bf16[128,64,128]{0,2,1:T(8,128)(2,1)}, u32[]{:S(2)}, u32[]{:S(2)}) %all-to-all-start) | async-done | bytes 2097184 | tf_op jit(solution)/shard_map/all_to_all | solution.py:80
  163.3 3.9 %copy.33 = bf16[16,128,4,128]{3,1,0,2:T(8,128)(2,1)} copy(bf16[16,128,4,128]{1,3,2,0:T(8,128)(2,1)} %bitcast.8) | data formatting | bytes 4194304 | tf_op jit(solution)/shard_map/all_to_all | solution.py:80
  168.9 80.4 %while.40 = (s32[]{:T(128)}, bf16[2048,4,128]{2,1,0:T(4,128)(2,1)}, s32[2048]{0:T(1024)S(1)}, bf16[2048,4,128]{2,0,1:T(8,128)(2,1)}, bf16[2048,4,128]{2,0,1:T(8,...) while((s32[]{:T(128)}, bf16[2048,4,128]{2,1,0:T(4,128)(2,1)}, ...), condition=%wide.region_7.8_spmd, body=%wide.region_2.7_spmd.sunk | while | flops 552342528 | bytes 30579452 | solution.py:66
  173.9 6.2 %while.41 = (s32[]{:T(128)}, f32[4,512]{1,0:T(4,128)S(1)}, f32[4,512]{1,0:T(4,128)S(1)}, f32[4,512,128]{2,1,0:T(8,128)}, s32[]{:T(128)}, /*index=5*/s32[512]{0:T...) while((s32[]{:T(128)}, f32[4,512]{1,0:T(4,128)S(1)}, ...), condition=%wide.region_6.6_spmd.clone, body=%wide.region_3.5_spmd.clone.sunk | while | flops 551818240 | bytes 25831676 | solution.py:54
  176.2 2.9 fusion.34
  187.9 12.3 %while.41 = (s32[]{:T(128)}, f32[4,512]{1,0:T(4,128)S(1)}, f32[4,512]{1,0:T(4,128)S(1)}, f32[4,512,128]{2,1,0:T(8,128)}, s32[]{:T(128)}, /*index=5*/s32[512]{0:T...) while((s32[]{:T(128)}, f32[4,512]{1,0:T(4,128)S(1)}, ...), condition=%wide.region_6.6_spmd.clone, body=%wide.region_3.5_spmd.clone.sunk | while | flops 551818240 | bytes 25831676 | solution.py:54
  190.2 2.9 fusion.34
  196.4 2.9 fusion.34
  208.1 18.4 %while.41 = (s32[]{:T(128)}, f32[4,512]{1,0:T(4,128)S(1)}, f32[4,512]{1,0:T(4,128)S(1)}, f32[4,512,128]{2,1,0:T(8,128)}, s32[]{:T(128)}, /*index=5*/s32[512]{0:T...) while((s32[]{:T(128)}, f32[4,512]{1,0:T(4,128)S(1)}, ...), condition=%wide.region_6.6_spmd.clone, body=%wide.region_3.5_spmd.clone.sunk | while | flops 551818240 | bytes 25831676 | solution.py:54
  210.3 2.9 fusion.34
  216.4 2.9 fusion.34
  222.6 2.9 fusion.34
  234.3 12.2 %while.41 = (s32[]{:T(128)}, f32[4,512]{1,0:T(4,128)S(1)}, f32[4,512]{1,0:T(4,128)S(1)}, f32[4,512,128]{2,1,0:T(8,128)}, s32[]{:T(128)}, /*index=5*/s32[512]{0:T...) while((s32[]{:T(128)}, f32[4,512]{1,0:T(4,128)S(1)}, ...), condition=%wide.region_6.6_spmd.clone, body=%wide.region_3.5_spmd.clone.sunk | while | flops 551818240 | bytes 25831676 | solution.py:54
  236.5 2.9 fusion.34
  242.7 2.9 fusion.34
  249.3 52.0 %all_to_all.69 = bf16[2048,4,128]{2,1,0:T(4,128)(2,1)S(1)} all-to-all(bf16[2048,4,128]{2,1,0:T(4,128)(2,1)} %get-tuple-element.137), channel_id=1, replica_groups=mesh['rep'=2,'head'=16] {'head'}, dimensions={0} | all-to-all | bytes 4194304 | tf_op jit(solution)/shard_map/all_to_all | solution.py:87
  303.8 4.5 %reshape.110 = bf16[1,128,8192]{2,1,0:T(8,128)(2,1)} reshape(bf16[128,16,4,128]{3,2,1,0:T(4,128)(2,1)} %copy.39) | data formatting | bytes 4194304 | tf_op jit(solution)/shard_map/reshape | solution.py:88
  (137 shorter events, 58.8 us)
Async XLA Ops:
  0.0 9.4 %copy-start.3 = (bf16[1,128,1024]{2,1,0:T(8,128)(2,1)S(1)}, bf16[1,128,1024]{2,1,0:T(8,128)(2,1)}, u32[]{:S(2)}) copy-start(bf16[1,128,1024]{2,1,0:T(8,128)(2,1)} %param.10) | copy-start | bytes 786436
  2.9 53.6 %all-to-all-start.1 = ((bf16[128,64,128]{2,0,1:T(8,128)(2,1)}), bf16[128,64,128]{2,0,1:T(8,128)(2,1)S(1)}, u32[]{:S(2)}, u32[]{:S(2)}) async-start(bf16[128,64,128]{2,0,1:T(8,128)(2,1)} %bitcast.60), calls=%async_computation.1 | async-start | bytes 4194304 | tf_op jit(solution)/shard_map/all_to_all | solution.py:81
  56.5 11.2 %copy-start.2 = (bf16[128,64,128]{2,0,1:T(8,128)(2,1)}, bf16[128,64,128]{2,0,1:T(8,128)(2,1)S(1)}, u32[]{:S(2)}) copy-start(bf16[128,64,128]{2,0,1:T(8,128)(2,1)S(1)} %all-to-all-done.1) | copy-start | bytes 6291460
  58.5 52.4 %all-to-all-start.2 = ((bf16[128,64,128]{2,0,1:T(8,128)(2,1)}), bf16[128,64,128]{2,0,1:T(8,128)(2,1)}, u32[]{:S(2)}, u32[]{:S(2)}) async-start(bf16[128,64,128]{2,0,1:T(8,128)(2,1)} %bitcast.61), calls=%async_computation.2 | async-start | bytes 4194304 | tf_op jit(solution)/shard_map/all_to_all | solution.py:82
  63.7 52.4 %copy-start.4 = (s32[1,8]{1,0:T(1,128)S(1)}, s32[1,8]{1,0:T(1,128)}, u32[]{:S(2)}) copy-start(s32[1,8]{1,0:T(1,128)} %param.11) | copy-start | bytes 100
  110.9 52.4 %all-to-all-start = ((bf16[128,64,128]{0,2,1:T(8,128)(2,1)}), bf16[128,64,128]{0,2,1:T(8,128)(2,1)}, u32[]{:S(2)}, u32[]{:S(2)}) async-start(bf16[128,64,128]{0,2,1:T(8,128)(2,1)} %bitcast.59), calls=%async_computation | async-start | bytes 4194304 | tf_op jit(solution)/shard_map/all_to_all | solution.py:80
  174.2 2.0 copy-start
  179.1 1.0 copy-start.1
  188.2 2.0 copy-start
  193.1 1.0 copy-start.1
  194.3 2.0 copy-start
  199.2 1.0 copy-start.1
  208.3 2.0 copy-start
  213.2 1.0 copy-start.1
  214.5 2.0 copy-start
  219.3 1.0 copy-start.1
  220.6 2.0 copy-start
  225.4 1.0 copy-start.1
  234.6 2.0 copy-start
  239.4 1.0 copy-start.1
  240.7 2.0 copy-start
  245.5 1.0 copy-start.1
where the time goes:
time: 311 us; the launch traced here: 308 us
  waiting for transfers between devices  132 us (42%)
  blocking collectives  52 us (17%)
  local copies, waits for them, and re-layouts  50.1 us (16%)
  matrix products  30 us (10%)
  other arithmetic  17.2 us (6%)
  starting transfers between devices  16.9 us (5%)
  loops' own time  9.88 us (3%)
    all_to_all x1, blocking collectives, local(): lax.all_to_all(outputs, 'head', split_axis=0, concat_axis=1, tiled=True)  52 us
    all_to_all x1, waiting for transfers between devices, local(): lax.all_to_all(k_heads, 'head', split_axis=1, concat_axis=0, tiled=True)  47 us
    all_to_all x1, waiting for transfers between devices, local(): lax.all_to_all(v_heads, 'head', split_axis=1, concat_axis=0, tiled=True)  43.2 us
    all_to_all x1, waiting for transfers between devices, local(): lax.all_to_all(q_heads, 'head', split_axis=1, concat_axis=0, tiled=True)  41.9 us
    dot_general x8, matrix products, visit(): jnp.einsum('hqk,khd->hqd', weights.astype(jnp.bfloat16), v_block, preferr...  22.9 us
    another operation x1, loops' own time, attend_range(): return lax.fori_loop(lower, upper, place, blank)  9.33 us
    reduce_sum x8, other arithmetic, visit(): total = total * factor + jnp.sum(weights, axis=2)  8.32 us
    while x40, local copies, waits for them, and re-layouts  7.84 us
  transfers between devices with their start and end apart: 3, of which 3 were waited for; matrix products, arithmetic and copies ran while one was open for 3% of the time, Pallas kernels for 0%

commit v1 on v0

v1 whole, which is shorter than its diff:
```python
import functools
import math

import jax
import jax.numpy as jnp
from jax import lax
from jax.experimental import pallas as pl
from jax.experimental.pallas import tpu as pltpu
from jax.sharding import PartitionSpec as P

Q_HEADS = 64
KV_HEADS = 8
HEAD_DIM = 128
GROUP = Q_HEADS // KV_HEADS
BIG = -1e30
FAR = 1 << 29
SCALE = float(HEAD_DIM) ** -0.5 * math.log2(math.e)
ROWS = 256
LOWEST, HIGHEST = 2.0 ** -40, 2.0 ** 100


def fill(slots, kv_refs, ka, va, core, tok):
    d = HEAD_DIM
    for at, arrays in slots:
        def copy(ref, at=at):
            ka[at * tok:(at + 1) * tok, :d] = ref[0]
            va[at * tok:(at + 1) * tok, :d] = ref[1]
        if len(arrays) == 1:
            copy(kv_refs[arrays[0]])
        else:
            for pick, array in enumerate(arrays):
                pl.when(core == pick)(functools.partial(copy, kv_refs[array]))


def prepare(info, total, docs, qa, ka, va, tok):
    d = HEAD_DIM
    q_pos = info[total] + lax.broadcasted_iota(jnp.int32, (tok, tok), 1)
    start = jnp.zeros((tok, tok), jnp.int32)
    end = jnp.int32(0)
    for doc in range(docs):
        length = info[total + 3 + doc]
        end = end + length
        start = start + jnp.where(q_pos >= end, length, 0)
    row = lax.broadcasted_iota(jnp.int32, (tok, tok), 0)
    for b in range(total):
        k_pos = info[b] + row
        allowed = (k_pos <= q_pos) & (k_pos >= start)
        ka[b * tok:(b + 1) * tok, d:] = jnp.where(allowed, 0.0, BIG).astype(jnp.bfloat16)
    one = (row == lax.broadcasted_iota(jnp.int32, (tok, tok), 1)).astype(jnp.float32)
    for j in range(GROUP):
        qa[j * tok:(j + 1) * tok, d:] = one.astype(jnp.bfloat16)
    va[:, d:] = jnp.ones((total * tok, d), jnp.bfloat16)


def scores(qa, ka, first, rows, low, high):
    return lax.dot_general(qa[first:first + rows, :], ka[low:high, :], (((1,), (1,)), ((), ())),
                           preferred_element_type=jnp.float32)


def sums(qa, ka, va, low, high, tok, take):
    ahead = scores(qa, ka, 0, ROWS, low, high)
    for first in range(0, GROUP * tok, ROWS):
        s = ahead
        if first + ROWS < GROUP * tok:
            ahead = scores(qa, ka, first + ROWS, ROWS, low, high)
        p = jnp.exp2(s * SCALE).astype(jnp.bfloat16)
        o = jnp.dot(p, va[low:high, :], preferred_element_type=jnp.float32)
        for j in range(ROWS // tok):
            take(first // tok + j, o[j * tok:(j + 1) * tok, :HEAD_DIM], o[j * tok:(j + 1) * tok, HEAD_DIM:])


def by_column(info, total, slots, cut, run):
    if cut is None:
        run(slots)
    else:
        column, count = cut
        pl.when(info[total + 1] == column)(lambda: run(slots[:count]))
        pl.when(info[total + 1] != column)(lambda: run(slots))


def early_kernel(total, slots, cut, docs, tok, info, q_ref, *rest):
    kv_refs, (acc_ref, sum_ref, qa, ka, va) = rest[:-5], rest[-5:]
    d = HEAD_DIM
    pl.when(pl.program_id(0) == 0)(lambda: prepare(info, total, docs, qa, ka, va, tok))
    for j in range(GROUP):
        qa[j * tok:(j + 1) * tok, :d] = q_ref[:, j * d:(j + 1) * d]

    def run(part):
        fill(part, kv_refs, ka, va, info[total + 2], tok)
        lane = lax.broadcasted_iota(jnp.int32, (tok, d), 1)
        packed = [jnp.zeros((tok, d), jnp.float32)]

        def take(j, acc, row_sum):
            acc_ref[:, j * d:(j + 1) * d] = acc
            packed[0] = jnp.where(lane == j, row_sum, packed[0])

        sums(qa, ka, va, part[0][0] * tok, (part[-1][0] + 1) * tok, tok, take)
        sum_ref[...] = packed[0]

    by_column(info, total, slots, cut, run)


def late_kernel(total, early, slots, cut, docs, tok, info, q_ref, acc_ref, sum_ref, *rest):
    kv_refs, (o_ref, qa, ka, va, bad) = rest[:-5], rest[-5:]
    d = HEAD_DIM
    pl.when(pl.program_id(0) == 0)(lambda: prepare(info, total, docs, qa, ka, va, tok))
    for j in range(GROUP):
        qa[j * tok:(j + 1) * tok, :d] = q_ref[:, j * d:(j + 1) * d]
    core = info[total + 2]

    def run(part):
        fill(part, kv_refs, ka, va, core, tok)
        off = [jnp.zeros((tok, d), jnp.float32)]

        def take(j, acc, row_sum):
            row_sum = row_sum + sum_ref[:, j:j + 1]
            fine = (row_sum >= LOWEST) & (row_sum <= HIGHEST)
            off[0] = jnp.where(fine, off[0], 1.0)
            o_ref[:, j * d:(j + 1) * d] = ((acc + acc_ref[:, j * d:(j + 1) * d]) / row_sum).astype(jnp.bfloat16)

        sums(qa, ka, va, part[0][0] * tok, (part[-1][0] + 1) * tok, tok, take)
        bad[...] = jnp.max(off[0], axis=0, keepdims=True)

    by_column(info, total, slots, cut, run)

    @pl.when(jnp.max(bad[...]) > 0.0)
    def _():
        fill(early + slots, kv_refs, ka, va, core, tok)
        for j in range(GROUP):
            s = scores(qa, ka, j * tok, tok, 0, total * tok)
            top = jnp.max(s, axis=1, keepdims=True)
            p = jnp.exp2((s - top) * SCALE).astype(jnp.bfloat16)
            o = jnp.dot(p, va[...], preferred_element_type=jnp.float32)
            o_ref[:, j * d:(j + 1) * d] = (o[:, :d] / o[:, d:]).astype(jnp.bfloat16)


def attend(body, q, state, arrays, info, total, keys, outs, scratch):
    tok = q.shape[0]
    d = HEAD_DIM
    wide = pl.BlockSpec((tok, GROUP * d), lambda g, info: (0, g))
    thin = pl.BlockSpec((None, tok, d), lambda g, info: (g, 0, 0))
    narrow = pl.BlockSpec((2, tok, d), lambda g, info: (0, 0, g))
    grid_spec = pltpu.PrefetchScalarGridSpec(
        num_scalar_prefetch=1,
        grid=(KV_HEADS,),
        in_specs=[wide] + [wide, thin][:len(state)] + [narrow] * len(arrays),
        out_specs=[wide, thin][:len(outs)],
        scratch_shapes=[
            pltpu.VMEM((GROUP * tok, 2 * d), jnp.bfloat16),
            pltpu.VMEM((total * tok, 2 * d), jnp.bfloat16),
            pltpu.VMEM((total * tok, 2 * d), jnp.bfloat16),
        ] + scratch,
    )
    return pl.pallas_call(
        body,
        out_shape=outs,
        grid_spec=grid_spec,
        compiler_params=pltpu.CompilerParams(vmem_limit_bytes=(24 if total <= 16 else 44) * 1024 * 1024),
        cost_estimate=pl.CostEstimate(flops=8 * Q_HEADS * tok * keys * d,
                                      bytes_accessed=4 * q.size + 4 * keys * KV_HEADS * d,
                                      transcendentals=Q_HEADS * tok * keys),
    )(info, q, *state, *arrays)


class Route:
    def __init__(self, devices):
        self.plane = math.isqrt(devices)
        self.cols = self.plane // 2
        self.levels = devices // self.plane
        self.reach = devices // 2 // self.plane

    def at(self, z, x, c):
        return z * self.plane + x * 2 + c

    def everyone(self, level, cores=(0, 1)):
        return [(z, x, c) for z in range(level, self.levels) for x in range(self.cols) for c in cores]

    def wanted(self, level, src, dst):
        return src < dst if level == 0 else src > dst if level == self.reach else True

    def up(self, level):
        return [(self.at(z - 1, x, c), self.at(z, x, c)) for z, x, c in self.everyone(level)]

    def across(self, level, dx, cores=(0, 1)):
        return [(self.at(z, (x - dx) % self.cols, c), self.at(z, x, c)) for z, x, c in self.everyone(level, cores)
                if self.wanted(level, (x - dx) % self.cols, x)]

    def climb(self, dx, cores):
        return [(self.at(z - 1, x, c), self.at(z, x, c)) for z, x, c in self.everyone(self.reach, cores)
                if self.wanted(self.reach, (x - dx) % self.cols, x)]

    def over(self, level, dx, cores=(0, 1)):
        return [(self.at(z, x, 1 - c), self.at(z, x, c)) for z, x, c in self.everyone(level, cores)
                if (self.wanted(level, 1 - c, c) if dx == 0 else self.wanted(level, (x - dx) % self.cols, x))]

    def carry(self, block, attend_early):
        send = lambda array, pairs: lax.ppermute(array, "head", pairs)
        reach, columns = self.reach, range(1, self.cols)
        got = {(0, 0, 0): [block]}

        def swap(level, dx):
            got[level, dx, 1] = [send(got[level, dx, 0][0], self.over(level, dx))]

        state = None
        for level in range(reach):
            held = got[level, 0, 0][0]
            new = [send(held, self.up(level + 1))]
            new += [send(held, self.across(level, dx)) for dx in columns]
            if level:
                for dx in columns:
                    swap(level - 1, dx)
                swap(level, 0)
                if level == 1:
                    state = attend_early(got)
                    new, state = lax.optimization_barrier((new, state))
            else:
                swap(0, 0)
            if level != 1:
                new = lax.optimization_barrier(new)
            got[level + 1, 0, 0] = [new[0]]
            for dx in columns:
                got[level, dx, 0] = [new[dx]]
        for dx in columns:
            got[reach, dx, 0] = [send(got[reach, 0, 0][0], self.across(reach, dx, (0,))),
                                 send(got[reach - 1, dx, 0][0], self.climb(dx, (1,)))]
        swap(reach, 0)
        for dx in columns:
            swap(reach - 1, dx)
            got[reach, dx, 1] = [send(got[reach, dx, 0][1 - c], self.over(reach, dx, (c,))) for c in range(2)]
        return got, state

    def order(self):
        names = [(level, dx, other) for dx in range(self.cols) for level in range(self.reach + 1) for other in range(2)]
        early = [n for n in names if n[0] == 0 or (n[0] == 1 and n[1] == 0 and self.reach > 1)]
        late = [n for n in names if n not in early]
        partial = lambda n: n[1] > 0 and n[0] in (0, self.reach)
        return sorted(early, key=partial), sorted(late, key=partial)

    def block(self, name, me):
        level, dx, other = name
        z, x, c = me // self.plane, me % self.plane // 2, me % 2
        col = (x - dx + self.cols) % self.cols
        core = 1 - c if other else c
        want = self.wanted(level, core, c) if dx == 0 else self.wanted(level, col, x)
        held = (z >= level) & (want | (dx == 0 and other == 0))
        return jnp.where(held, self.at(z - level, col, core), -1)


def local(query, key, value, lengths):
    tok = query.shape[1]
    docs = lengths.shape[1]
    d = HEAD_DIM
    me = lax.axis_index("head")
    route = Route(lax.axis_size("head"))
    early, late = route.order()
    total = len(early) + len(late)
    base = [jnp.where(b >= 0, b * tok, FAR) for b in (route.block(name, me) for name in early + late)]
    info = jnp.stack(base + [me * tok, me % route.plane // 2, me % 2])
    info = jnp.concatenate([info, lengths[0]]).astype(jnp.int32)

    q = query[0]
    cut = (lambda column, part: (column, len(part) - 2)) if route.cols == 2 else (lambda column, part: None)

    def listed(got, names, at):
        arrays, slots = [], []
        for name in names:
            slots.append((at + len(slots), list(range(len(arrays), len(arrays) + len(got[name])))))
            arrays += got[name]
        return arrays, slots

    def attend_early(got):
        arrays, slots = listed(got, early, 0)
        return attend(
            functools.partial(early_kernel, total, slots, cut(0, slots), docs, tok), q, [], arrays, info, total,
            len(slots) * tok,
            [jax.ShapeDtypeStruct(q.shape, jnp.float32), jax.ShapeDtypeStruct((KV_HEADS, tok, d), jnp.float32)], [])

    got, state = route.carry(jnp.stack([key[0], value[0]]), attend_early)
    arrays, slots = listed(got, early + late, 0)
    first, last = slots[:len(early)], slots[len(early):]
    out, = attend(
        functools.partial(late_kernel, total, first, last, cut(1, last), docs, tok), q, state, arrays, info, total,
        len(last) * tok, [jax.ShapeDtypeStruct(q.shape, jnp.bfloat16)], [pltpu.VMEM((1, d), jnp.float32)])
    return out[None]


def solution(mesh):
    placed = (
        P("rep", "head", None),
        P("rep", "head", None),
        P("rep", "head", None),
        P("rep", None),
    )
    return jax.shard_map(
        local, mesh=mesh, in_specs=placed, out_specs=P("rep", "head", None), check_vma=False
    )
```

time: 311 us -> 113 us (0.36)
  waiting for transfers between devices: 132 us -> 14.4 us
  Pallas kernels: 0 us -> 62.3 us
  blocking collectives: 52 us -> 0 us
  local copies, waits for them, and re-layouts: 50.1 us -> 4.27 us
  matrix products: 30 us -> 0 us
  other arithmetic: 17.2 us -> 0 us
  starting transfers between devices: 16.9 us -> 31.7 us
  loops' own time: 9.88 us -> 0 us
    all_to_all x3 -> x0, waiting for transfers between devices: 132 us -> none  [the longest x1 47 us: local(): lax.all_to_all(k_heads, 'head', split_axis=1, concat_axis=0, tiled=True)]
    pallas_call x0 -> x2, Pallas kernels: none -> 62.3 us  [attend(): pl.pallas_call(body, out_shape=outs, grid_spec=grid_spec, compiler_params...]
    all_to_all x1 -> x0, blocking collectives: 52 us -> none  [local(): lax.all_to_all(outputs, 'head', split_axis=0, concat_axis=1, tiled=True)]
    ppermute x0 -> x13, starting transfers between devices: none -> 31.7 us  [carry(): send = lambda array, pairs: lax.ppermute(array, 'head', pairs)]
    dot_general x16 -> x0, matrix products: 30 us -> none  [the longest x8 22.9 us: visit(): jnp.einsum('hqk,khd->hqd', weights.astype(jnp.bfloat16), v_block, preferr...]
    all_to_all x3 -> x0, starting transfers between devices: 16.9 us -> none  [the longest x1 6.47 us: local(): lax.all_to_all(k_heads, 'head', split_axis=1, concat_axis=0, tiled=True)]
    ppermute x0 -> x13, waiting for transfers between devices: none -> 14.4 us  [carry(): send = lambda array, pairs: lax.ppermute(array, 'head', pairs)]
    all_to_all x4 -> x0, local copies, waits for them, and re-layouts: 11.4 us -> none  [the longest x1 3.93 us: local(): lax.all_to_all(q_heads, 'head', split_axis=1, concat_axis=0, tiled=True)]
  transfers between devices with their start and end apart: 3 -> 13, of which waited for: 3 -> 5; matrix products, arithmetic and copies ran while one was open for 3% -> 1% of each run, Pallas kernels for 0% -> 8%
where the time goes in v1:
time: 113 us
  Pallas kernels  62.3 us (55%)
  starting transfers between devices  31.7 us (28%)
  waiting for transfers between devices  14.4 us (13%)
  local copies, waits for them, and re-layouts  4.27 us (4%)
    pallas_call x2, Pallas kernels, attend(): pl.pallas_call(body, out_shape=outs, grid_spec=grid_spec, compiler_params...  62.3 us
    ppermute x13, starting transfers between devices, carry(): send = lambda array, pairs: lax.ppermute(array, 'head', pairs)  31.7 us
    ppermute x13, waiting for transfers between devices, carry(): send = lambda array, pairs: lax.ppermute(array, 'head', pairs)  14.4 us
    unnamed x3, local copies, waits for them, and re-layouts  2.55 us
  transfers between devices with their start and end apart: 13, of which 5 were waited for; matrix products, arithmetic and copies ran while one was open for 1% of the time, Pallas kernels for 8%

profile of v1, /device:TPU:17, one launch (start us, length us, event | category | flops | bytes accessed | tf_op | source)
XLA Modules:
  0.0 112.9 jit_solution(17049852178218786219)
XLA Ops:
  0.0 1.0 constant_dynamic-update-slice_fusion.1
  1.0 1.0 constant_dynamic-update-slice_fusion.rest_0_
  1.9 3.1 %collective-permute-start.1 = (bf16[2,128,1024]{2,1,0:T(8,128)(2,1)S(1)}, bf16[2,128,1024]{2,1,0:T(8,128)(2,1)S(1)}, u32[]{:S(2)}, u32[]{:S(2)}) collective-permute-start(bf16[2,128,1024]{2,1,0:T(8,128)(2,1)S(1)} %constant_dynamic-update-slice_fusion.rest_0_), channel_id=1, source_target_pairs={{0,2},{1,3},{4,6},{5,7},{8,10},{9,11},{12,14},{13,15},{16,18},{17,... | collective-permute-start | bytes 1572872 | tf_op jit(solution)/shard_map/ppermute | solution.py:197
  5.1 3.2 %collective-permute-start = (bf16[2,128,1024]{2,1,0:T(8,128)(2,1)S(1)}, bf16[2,128,1024]{2,1,0:T(8,128)(2,1)S(1)}, u32[]{:S(2)}, u32[]{:S(2)}) collective-permute-start(bf16[2,128,1024]{2,1,0:T(8,128)(2,1)S(1)} %constant_dynamic-update-slice_fusion.rest_0_), channel_id=1, source_target_pairs={{0,4},{1,5},{2,6},{3,7},{4,8},{5,9},{6,10},{7,11},{8,12},{9,13},{1... | collective-permute-start | bytes 1572872 | tf_op jit(solution)/shard_map/ppermute | solution.py:197
  8.3 1.3 %collective-permute-start.4 = (bf16[2,128,1024]{2,1,0:T(8,128)(2,1)S(1)}, bf16[2,128,1024]{2,1,0:T(8,128)(2,1)S(1)}, u32[]{:S(2)}, u32[]{:S(2)}) collective-permute-start(bf16[2,128,1024]{2,1,0:T(8,128)(2,1)S(1)} %constant_dynamic-update-slice_fusion.rest_0_), channel_id=1, source_target_pairs={{0,1},{2,3},{4,5},{6,7},{8,9},{10,11},{12,13},{14,15},{16,17},{18,... | collective-permute-start | bytes 1572872 | tf_op jit(solution)/shard_map/ppermute | solution.py:197
  9.6 6.0 %collective-permute-done.1.rest_4_ = bf16[2,128,1024]{2,1,0:T(8,128)(2,1)S(1)} collective-permute-done((bf16[2,128,1024]{2,1,0:T(8,128)(2,1)S(1)}, bf16[2,128,1024]{2,1,0:T(8,128)(2,1)S(1)}, u32[]{:S(2)}, u32[]{:S(2)}) %collective-permute-start.1) | collective-permute-done | bytes 524320 | tf_op jit(solution)/shard_map/ppermute | solution.py:197
  15.6 3.8 %collective-permute-done.rest_2_ = bf16[2,128,1024]{2,1,0:T(8,128)(2,1)S(1)} collective-permute-done((bf16[2,128,1024]{2,1,0:T(8,128)(2,1)S(1)}, bf16[2,128,1024]{2,1,0:T(8,128)(2,1)S(1)}, u32[]{:S(2)}, u32[]{:S(2)}) %collective-permute-start) | collective-permute-done | bytes 524320 | tf_op jit(solution)/shard_map/ppermute | solution.py:197
  19.5 0.7 collective-permute-start.6
  20.2 3.8 %collective-permute-start.5 = (bf16[2,128,1024]{2,1,0:T(8,128)(2,1)S(1)}, bf16[2,128,1024]{2,1,0:T(8,128)(2,1)S(1)}, u32[]{:S(2)}, u32[]{:S(2)}) collective-permute-start(bf16[2,128,1024]{2,1,0:T(8,128)(2,1)S(1)} %collective-permute-done.rest_2_), channel_id=1, source_target_pairs={{5,4},{4,5},{7,6},{6,7},{9,8},{8,9},{11,10},{10,11},{13,12},{12,13... | collective-permute-start | bytes 1572872 | tf_op jit(solution)/shard_map/ppermute | solution.py:197
  24.1 0.7 concatenate.3.info
  24.9 2.5 %collective-permute-start.3 = (bf16[2,128,1024]{2,1,0:T(8,128)(2,1)S(1)}, bf16[2,128,1024]{2,1,0:T(8,128)(2,1)S(1)}, u32[]{:S(2)}, u32[]{:S(2)}) collective-permute-start(bf16[2,128,1024]{2,1,0:T(8,128)(2,1)S(1)} %collective-permute-done.rest_2_), channel_id=1, source_target_pairs={{6,4},{7,5},{4,6},{5,7},{10,8},{11,9},{8,10},{9,11},{14,12},{15,13... | collective-permute-start | bytes 1572872 | tf_op jit(solution)/shard_map/ppermute | solution.py:197
  27.4 3.2 %collective-permute-start.2 = (bf16[2,128,1024]{2,1,0:T(8,128)(2,1)S(1)}, bf16[2,128,1024]{2,1,0:T(8,128)(2,1)S(1)}, u32[]{:S(2)}, u32[]{:S(2)}) collective-permute-start(bf16[2,128,1024]{2,1,0:T(8,128)(2,1)S(1)} %collective-permute-done.rest_2_), channel_id=1, source_target_pairs={{4,8},{5,9},{6,10},{7,11},{8,12},{9,13},{10,14},{11,15},{20,24},{2... | collective-permute-start | bytes 1572872 | tf_op jit(solution)/shard_map/ppermute | solution.py:197
  30.6 1.6 %copy-done = bf16[1,128,8192]{2,1,0:T(8,128)(2,1)S(1)} copy-done((bf16[1,128,8192]{2,1,0:T(8,128)(2,1)S(1)}, bf16[1,128,8192]{2,1,0:T(8,128)(2,1)}, u32[]{:S(2)}) %copy-start) | copy-done | bytes 2097176
  32.2 8.8 %shard_map.46 = (f32[128,8192]{1,0:T(8,128)S(1)}, f32[8,128,128]{2,1,0:T(8,128)S(1)}) custom-call(s32[23]{0:T(128)S(1)} %concatenate.3.info, bf16[128,8192]{1,0:T(8,128)(2,1)S(1)} %bitcast.18, bf16[2,128,1024]{2,1,0:T(8,128)(2,1)S(1)} %constant_dynamic-update-slice_fusion.rest_0_, bf16[2,128,1024]{2,1,0:T(8,128)(2,1)S(1)} %collective-permute-done.4.rest_1_, ...), custom_call_target="tpu_custom_call" | custom-call | flops 6442450944 | bytes 7340032 | tf_op jit(solution)/shard_map/pallas_call | solution.py:154
  41.0 1.0 collective-permute-done.2.rest_6_
  41.9 0.7 collective-permute-start.9
  42.6 3.2 %collective-permute-start.10 = (bf16[2,128,1024]{2,1,0:T(8,128)(2,1)S(1)}, bf16[2,128,1024]{2,1,0:T(8,128)(2,1)S(1)}, u32[]{:S(2)}, u32[]{:S(2)}) collective-permute-start(bf16[2,128,1024]{2,1,0:T(8,128)(2,1)S(1)} %collective-permute-done.3.rest_8_), channel_id=1, source_target_pairs={{5,9},{9,13},{21,25},{25,29}} | collective-permute-start | bytes 1572872 | tf_op jit(solution)/shard_map/ppermute | solution.py:197
  45.8 1.7 %collective-permute-start.7 = (bf16[2,128,1024]{2,1,0:T(8,128)(2,1)S(1)}, bf16[2,128,1024]{2,1,0:T(8,128)(2,1)S(1)}, u32[]{:S(2)}, u32[]{:S(2)}) collective-permute-start(bf16[2,128,1024]{2,1,0:T(8,128)(2,1)S(1)} %collective-permute-done.2.rest_6_), channel_id=1, source_target_pairs={{9,8},{11,10},{13,12},{15,14},{25,24},{27,26},{29,28},{31,30}} | collective-permute-start | bytes 1572872 | tf_op jit(solution)/shard_map/ppermute | solution.py:197
  47.5 1.9 %collective-permute-start.8 = (bf16[2,128,1024]{2,1,0:T(8,128)(2,1)S(1)}, bf16[2,128,1024]{2,1,0:T(8,128)(2,1)S(1)}, u32[]{:S(2)}, u32[]{:S(2)}) collective-permute-start(bf16[2,128,1024]{2,1,0:T(8,128)(2,1)S(1)} %collective-permute-done.3.rest_8_), channel_id=1, source_target_pairs={{5,4},{4,5},{7,6},{6,7},{9,8},{8,9},{11,10},{10,11},{13,12},{12,13... | collective-permute-start | bytes 1572872 | tf_op jit(solution)/shard_map/ppermute | solution.py:197
  49.5 1.3 %collective-permute-start.12 = (bf16[2,128,1024]{2,1,0:T(8,128)(2,1)S(1)}, bf16[2,128,1024]{2,1,0:T(8,128)(2,1)S(1)}, u32[]{:S(2)}, u32[]{:S(2)}) collective-permute-start(bf16[2,128,1024]{2,1,0:T(8,128)(2,1)S(1)} %collective-permute-done.9.rest_10_), channel_id=1, source_target_pairs={{8,9},{12,13},{24,25},{28,29}} | collective-permute-start | bytes 1572872 | tf_op jit(solution)/shard_map/ppermute | solution.py:197
  50.8 2.1 %collective-permute-done.10.rest_11_ = bf16[2,128,1024]{2,1,0:T(8,128)(2,1)S(1)} collective-permute-done((bf16[2,128,1024]{2,1,0:T(8,128)(2,1)S(1)}, bf16[2,128,1024]{2,1,0:T(8,128)(2,1)S(1)}, u32[]{:S(2)}, u32[]{:S(2)}) %collective-permute-start.10) | collective-permute-done | bytes 524320 | tf_op jit(solution)/shard_map/ppermute | solution.py:197
  52.8 5.1 %collective-permute-start.11 = (bf16[2,128,1024]{2,1,0:T(8,128)(2,1)S(1)}, bf16[2,128,1024]{2,1,0:T(8,128)(2,1)S(1)}, u32[]{:S(2)}, u32[]{:S(2)}) collective-permute-start(bf16[2,128,1024]{2,1,0:T(8,128)(2,1)S(1)} %collective-permute-done.10.rest_11_), channel_id=1, source_target_pairs={{9,8},{13,12},{25,24},{29,28}} | collective-permute-start | bytes 1572872 | tf_op jit(solution)/shard_map/ppermute | solution.py:197
  58.0 1.5 %collective-permute-done.11.rest_12_ = bf16[2,128,1024]{2,1,0:T(8,128)(2,1)S(1)} collective-permute-done((bf16[2,128,1024]{2,1,0:T(8,128)(2,1)S(1)}, bf16[2,128,1024]{2,1,0:T(8,128)(2,1)S(1)}, u32[]{:S(2)}, u32[]{:S(2)}) %collective-permute-start.11) | collective-permute-done | bytes 524320 | tf_op jit(solution)/shard_map/ppermute | solution.py:197
  59.4 53.5 %shard_map.47 = bf16[128,8192]{1,0:T(8,128)(2,1)} custom-call(s32[23]{0:T(128)S(1)} %concatenate.3.info, bf16[128,8192]{1,0:T(8,128)(2,1)S(1)} %bitcast.19, f32[128,8192]{1,0:T(8,128)S(1)} %get-tuple-element.17.acc_ref, f32[8,128,128]{2,1,0:T(8,128)S(1)} %get-tuple-element.18.sum_ref, bf16[2,128,1024]{2,1,0:T(8,128)(2,1)S(1)} %constant_dynamic-update-slice_fusion.rest_0_, ...), custom_call_target="tpu_custom_call" | custom-call | flops 6442450944 | bytes 7340032 | tf_op jit(solution)/shard_map/pallas_call | solution.py:154
  (9 shorter events, 0.0 us)
Async XLA Ops:
  1.9 13.7 %collective-permute-start.1 = (bf16[2,128,1024]{2,1,0:T(8,128)(2,1)S(1)}, bf16[2,128,1024]{2,1,0:T(8,128)(2,1)S(1)}, u32[]{:S(2)}, u32[]{:S(2)}) collective-permute-start(bf16[2,128,1024]{2,1,0:T(8,128)(2,1)S(1)} %constant_dynamic-update-slice_fusion.rest_0_), channel_id=1, source_target_pairs={{0,2},{1,3},{4,6},{5,7},{8,10},{9,11},{12,14},{13,15},{16,18},{17,... | collective-permute-start | bytes 1572872 | tf_op jit(solution)/shard_map/ppermute | solution.py:197
  5.1 14.4 %collective-permute-start = (bf16[2,128,1024]{2,1,0:T(8,128)(2,1)S(1)}, bf16[2,128,1024]{2,1,0:T(8,128)(2,1)S(1)}, u32[]{:S(2)}, u32[]{:S(2)}) collective-permute-start(bf16[2,128,1024]{2,1,0:T(8,128)(2,1)S(1)} %constant_dynamic-update-slice_fusion.rest_0_), channel_id=1, source_target_pairs={{0,4},{1,5},{2,6},{3,7},{4,8},{5,9},{6,10},{7,11},{8,12},{9,13},{1... | collective-permute-start | bytes 1572872 | tf_op jit(solution)/shard_map/ppermute | solution.py:197
  8.3 22.3 %collective-permute-start.4 = (bf16[2,128,1024]{2,1,0:T(8,128)(2,1)S(1)}, bf16[2,128,1024]{2,1,0:T(8,128)(2,1)S(1)}, u32[]{:S(2)}, u32[]{:S(2)}) collective-permute-start(bf16[2,128,1024]{2,1,0:T(8,128)(2,1)S(1)} %constant_dynamic-update-slice_fusion.rest_0_), channel_id=1, source_target_pairs={{0,1},{2,3},{4,5},{6,7},{8,9},{10,11},{12,13},{14,15},{16,17},{18,... | collective-permute-start | bytes 1572872 | tf_op jit(solution)/shard_map/ppermute | solution.py:197
  19.5 11.1 %collective-permute-start.6 = (bf16[2,128,1024]{2,1,0:T(8,128)(2,1)S(1)}, bf16[2,128,1024]{2,1,0:T(8,128)(2,1)S(1)}, u32[]{:S(2)}, u32[]{:S(2)}) collective-permute-start(bf16[2,128,1024]{2,1,0:T(8,128)(2,1)S(1)} %collective-permute-done.1.rest_4_), channel_id=1, source_target_pairs={{3,2},{2,3},{7,6},{6,7},{11,10},{10,11},{15,14},{14,15},{19,18},{1... | collective-permute-start | bytes 1572872 | tf_op jit(solution)/shard_map/ppermute | solution.py:197
  20.2 10.4 %collective-permute-start.5 = (bf16[2,128,1024]{2,1,0:T(8,128)(2,1)S(1)}, bf16[2,128,1024]{2,1,0:T(8,128)(2,1)S(1)}, u32[]{:S(2)}, u32[]{:S(2)}) collective-permute-start(bf16[2,128,1024]{2,1,0:T(8,128)(2,1)S(1)} %collective-permute-done.rest_2_), channel_id=1, source_target_pairs={{5,4},{4,5},{7,6},{6,7},{9,8},{8,9},{11,10},{10,11},{13,12},{12,13... | collective-permute-start | bytes 1572872 | tf_op jit(solution)/shard_map/ppermute | solution.py:197
  24.9 16.1 %collective-permute-start.3 = (bf16[2,128,1024]{2,1,0:T(8,128)(2,1)S(1)}, bf16[2,128,1024]{2,1,0:T(8,128)(2,1)S(1)}, u32[]{:S(2)}, u32[]{:S(2)}) collective-permute-start(bf16[2,128,1024]{2,1,0:T(8,128)(2,1)S(1)} %collective-permute-done.rest_2_), channel_id=1, source_target_pairs={{6,4},{7,5},{4,6},{5,7},{10,8},{11,9},{8,10},{9,11},{14,12},{15,13... | collective-permute-start | bytes 1572872 | tf_op jit(solution)/shard_map/ppermute | solution.py:197
  27.4 14.6 %collective-permute-start.2 = (bf16[2,128,1024]{2,1,0:T(8,128)(2,1)S(1)}, bf16[2,128,1024]{2,1,0:T(8,128)(2,1)S(1)}, u32[]{:S(2)}, u32[]{:S(2)}) collective-permute-start(bf16[2,128,1024]{2,1,0:T(8,128)(2,1)S(1)} %collective-permute-done.rest_2_), channel_id=1, source_target_pairs={{4,8},{5,9},{6,10},{7,11},{8,12},{9,13},{10,14},{11,15},{20,24},{2... | collective-permute-start | bytes 1572872 | tf_op jit(solution)/shard_map/ppermute | solution.py:197
  30.6 1.6 %copy-start = (bf16[1,128,8192]{2,1,0:T(8,128)(2,1)S(1)}, bf16[1,128,8192]{2,1,0:T(8,128)(2,1)}, u32[]{:S(2)}) copy-start(bf16[1,128,8192]{2,1,0:T(8,128)(2,1)} %param.4) | copy-start | bytes 6291460
  41.9 7.5 %collective-permute-start.9 = (bf16[2,128,1024]{2,1,0:T(8,128)(2,1)S(1)}, bf16[2,128,1024]{2,1,0:T(8,128)(2,1)S(1)}, u32[]{:S(2)}, u32[]{:S(2)}) collective-permute-start(bf16[2,128,1024]{2,1,0:T(8,128)(2,1)S(1)} %collective-permute-done.2.rest_6_), channel_id=1, source_target_pairs={{10,8},{14,12},{26,24},{30,28}} | collective-permute-start | bytes 1572872 | tf_op jit(solution)/shard_map/ppermute | solution.py:197
  42.6 10.2 %collective-permute-start.10 = (bf16[2,128,1024]{2,1,0:T(8,128)(2,1)S(1)}, bf16[2,128,1024]{2,1,0:T(8,128)(2,1)S(1)}, u32[]{:S(2)}, u32[]{:S(2)}) collective-permute-start(bf16[2,128,1024]{2,1,0:T(8,128)(2,1)S(1)} %collective-permute-done.3.rest_8_), channel_id=1, source_target_pairs={{5,9},{9,13},{21,25},{25,29}} | collective-permute-start | bytes 1572872 | tf_op jit(solution)/shard_map/ppermute | solution.py:197
  45.8 12.1 %collective-permute-start.7 = (bf16[2,128,1024]{2,1,0:T(8,128)(2,1)S(1)}, bf16[2,128,1024]{2,1,0:T(8,128)(2,1)S(1)}, u32[]{:S(2)}, u32[]{:S(2)}) collective-permute-start(bf16[2,128,1024]{2,1,0:T(8,128)(2,1)S(1)} %collective-permute-done.2.rest_6_), channel_id=1, source_target_pairs={{9,8},{11,10},{13,12},{15,14},{25,24},{27,26},{29,28},{31,30}} | collective-permute-start | bytes 1572872 | tf_op jit(solution)/shard_map/ppermute | solution.py:197
  47.5 10.4 %collective-permute-start.8 = (bf16[2,128,1024]{2,1,0:T(8,128)(2,1)S(1)}, bf16[2,128,1024]{2,1,0:T(8,128)(2,1)S(1)}, u32[]{:S(2)}, u32[]{:S(2)}) collective-permute-start(bf16[2,128,1024]{2,1,0:T(8,128)(2,1)S(1)} %collective-permute-done.3.rest_8_), channel_id=1, source_target_pairs={{5,4},{4,5},{7,6},{6,7},{9,8},{8,9},{11,10},{10,11},{13,12},{12,13... | collective-permute-start | bytes 1572872 | tf_op jit(solution)/shard_map/ppermute | solution.py:197
  49.5 8.5 %collective-permute-start.12 = (bf16[2,128,1024]{2,1,0:T(8,128)(2,1)S(1)}, bf16[2,128,1024]{2,1,0:T(8,128)(2,1)S(1)}, u32[]{:S(2)}, u32[]{:S(2)}) collective-permute-start(bf16[2,128,1024]{2,1,0:T(8,128)(2,1)S(1)} %collective-permute-done.9.rest_10_), channel_id=1, source_target_pairs={{8,9},{12,13},{24,25},{28,29}} | collective-permute-start | bytes 1572872 | tf_op jit(solution)/shard_map/ppermute | solution.py:197
  52.8 6.6 %collective-permute-start.11 = (bf16[2,128,1024]{2,1,0:T(8,128)(2,1)S(1)}, bf16[2,128,1024]{2,1,0:T(8,128)(2,1)S(1)}, u32[]{:S(2)}, u32[]{:S(2)}) collective-permute-start(bf16[2,128,1024]{2,1,0:T(8,128)(2,1)S(1)} %collective-permute-done.10.rest_11_), channel_id=1, source_target_pairs={{9,8},{13,12},{25,24},{29,28}} | collective-permute-start | bytes 1572872 | tf_op jit(solution)/shard_map/ppermute | solution.py:197

commit v2 on v1

v2 whole, which is shorter than its diff:
```python
import functools
import math

import jax
import jax.numpy as jnp
from jax import lax
from jax.experimental import pallas as pl
from jax.experimental.pallas import tpu as pltpu
from jax.sharding import PartitionSpec as P

Q_HEADS = 64
KV_HEADS = 8
HEAD_DIM = 128
GROUP = Q_HEADS // KV_HEADS
BIG = -1e30
FAR = 1 << 29
SCALE = float(HEAD_DIM) ** -0.5 * math.log2(math.e)
UNIT = 2
TILE = 256
LOWEST, HIGHEST = 2.0 ** -40, 2.0 ** 100
COST = 16


def masks(slots, info, total, docs, tok):
    q_pos = info[total] + lax.broadcasted_iota(jnp.int32, (tok, tok), 1)
    start = jnp.zeros((tok, tok), jnp.int32)
    end = jnp.int32(0)
    for doc in range(docs):
        length = info[total + 2 + doc]
        end = end + length
        start = start + jnp.where(q_pos >= end, length, 0)
    row = lax.broadcasted_iota(jnp.int32, (tok, tok), 0)
    for at, _ in slots:
        k_pos = info[at] + row
        yield jnp.where((k_pos <= q_pos) & (k_pos >= start), 0.0, BIG).astype(jnp.bfloat16)


def scores(q, k):
    return lax.dot_general(q, k, (((1,), (1,)), ((), ())), preferred_element_type=jnp.float32)


def kernel(form, info, *refs):
    total, early, late, cut, docs, tok, rows, count, is_late = form
    d = HEAD_DIM
    wide = GROUP * d
    refs = list(refs)
    q_ref = refs.pop(0)
    state = [refs.pop(0), refs.pop(0)] if is_late else []
    kv_refs, refs = refs[:count], refs[count:]
    slots = late if is_late else early
    if is_late:
        out_ref, mask_ref, out_buf, limits, everything, sems = refs
    else:
        acc_ref, sum_ref, mask_ref = refs
    row = lax.broadcasted_iota(jnp.int32, (tok, tok), 0)
    eye = (row == lax.broadcasted_iota(jnp.int32, (tok, tok), 1)).astype(jnp.float32).astype(jnp.bfloat16)
    one = jnp.ones((tok, d), jnp.bfloat16)

    def span(g, width):
        return pl.ds(pl.multiple_of(g * width, width), width)

    def queries(g, first, rows):
        return jnp.concatenate([jnp.concatenate([q_ref[:, span(g * GROUP + j, d)], eye], axis=1)
                                for j in range(first // tok, (first + rows) // tok)], axis=0)

    def result(u, buf, h):
        return pltpu.make_async_copy(out_buf.at[buf, h], out_ref.at[:, span(u * UNIT + h, wide)], sems.at[buf, h])

    def attend(part, u, buf):
        keys = len(part) * tok
        lane = lax.broadcasted_iota(jnp.int32, (tok, d), 1)
        packed = [jnp.zeros((tok, d), jnp.float32) for _ in range(UNIT)]
        least = most = jnp.ones((tok, d), jnp.float32)
        pieces = [(h, first) for h in range(UNIT) for first in range(0, GROUP * tok, rows)]
        step = TILE // tok
        tiles = [range(low, min(low + step, len(part))) for low in range(0, len(part), step)]

        def score(piece, tile):
            g = u * UNIT + piece[0]
            k = [jnp.concatenate([kv_refs[part[n][1]][0, :, span(g, d)], mask_ref[n * tok:(n + 1) * tok, :]], axis=1)
                 for n in tile]
            return scores(queries(g, piece[1], rows), jnp.concatenate(k, axis=0))

        ahead = [score(pieces[0], tile) for tile in tiles]
        for i, (h, first) in enumerate(pieces):
            g = u * UNIT + h
            s, ahead, p = ahead, [], []
            for n, tile in enumerate(tiles):
                p.append(jnp.exp2(s[n] * SCALE).astype(jnp.bfloat16))
                if i + 1 < len(pieces):
                    ahead.append(score(pieces[i + 1], tile))
            v = [jnp.concatenate([kv_refs[array][1, :, span(g, d)], one], axis=1) for _, array in part]
            o = jnp.dot(jnp.concatenate(p, axis=1), jnp.concatenate(v, axis=0), preferred_element_type=jnp.float32)
            for n in range(rows // tok):
                j = first // tok + n
                acc, row_sum = o[n * tok:(n + 1) * tok, :d], o[n * tok:(n + 1) * tok, d:]
                if is_late:
                    row_sum = row_sum + state[1][g, :, j:j + 1]
                    least, most = jnp.minimum(least, row_sum), jnp.maximum(most, row_sum)
                    share = pl.reciprocal(row_sum, approx=True)
                    share = share * (2.0 - row_sum * share)
                    acc = (acc + state[0][:, span(g * GROUP + j, d)]) * share
                    out_buf[buf, h, :, j * d:(j + 1) * d] = acc.astype(jnp.bfloat16)
                else:
                    packed[h] = jnp.where(lane == j, row_sum, packed[h])
                    acc_ref[:, span(g * GROUP + j, d)] = acc
        if is_late:
            limits[0] = jnp.minimum(limits[0], least)
            limits[1] = jnp.maximum(limits[1], most)
        else:
            for h in range(UNIT):
                sum_ref[u * UNIT + h] = packed[h]

    def run(part):
        units = KV_HEADS // UNIT
        for n, mask in enumerate(masks(part, info, total, docs, tok)):
            mask_ref[n * tok:(n + 1) * tok, :] = mask
        if is_late:
            limits[...] = jnp.ones((2, tok, d), jnp.float32)

        def step(u, carry):
            buf = lax.rem(u, 2)
            if is_late:
                @pl.when(u > 1)
                def _():
                    for h in range(UNIT):
                        result(u - 2, buf, h).wait()
            attend(part, u, buf)
            if is_late:
                for h in range(UNIT):
                    result(u, buf, h).start()
            return carry

        lax.fori_loop(0, units, step, 0)
        if is_late:
            for u in range(units - 2, units):
                for h in range(UNIT):
                    result(u, u % 2, h).wait()

    if cut is None:
        run(slots)
    else:
        for column, picked in enumerate(cut):
            pl.when(info[total + 1] == column)(functools.partial(run, [slots[n] for n in picked]))

    if is_late:
        inside = (limits[0] >= LOWEST) & (limits[1] <= HIGHEST)

        @pl.when(jnp.max(jnp.where(inside, 0.0, 1.0)) > 0.0)
        def _():
            for n, mask in enumerate(masks(early + late, info, total, docs, tok)):
                everything[0, n * tok:(n + 1) * tok, d:] = mask
                everything[1, n * tok:(n + 1) * tok, d:] = one

            def again(g, carry):
                for n, (_, array) in enumerate(early + late):
                    copy = pltpu.make_async_copy(kv_refs[array].at[:, :, span(g, d)],
                                                 everything.at[:, n * tok:(n + 1) * tok, :d], sems.at[0, 0])
                    copy.start()
                    copy.wait()
                for j in range(GROUP):
                    s = scores(queries(g, j * tok, tok), everything[0])
                    top = jnp.max(s, axis=1, keepdims=True)
                    p = jnp.exp2((s - top) * SCALE).astype(jnp.bfloat16)
                    o = jnp.dot(p, everything[1], preferred_element_type=jnp.float32)
                    out_buf[0, 0, :, j * d:(j + 1) * d] = (o[:, :d] / o[:, d:]).astype(jnp.bfloat16)
                store = pltpu.make_async_copy(out_buf.at[0, 0], out_ref.at[:, span(g, wide)], sems.at[0, 0])
                store.start()
                store.wait()
                return carry

            lax.fori_loop(0, KV_HEADS, again, 0)


def attend(form, q, state, arrays, info, outs):
    total, early, late, cut, docs, tok, rows, count, is_late = form
    d = HEAD_DIM
    n = max(len(picked) for picked in cut) if cut else len(late if is_late else early)
    anywhere, here = pl.BlockSpec(memory_space=pl.ANY), pl.BlockSpec(memory_space=pltpu.VMEM)
    scratch = [pltpu.VMEM((n * tok, d), jnp.bfloat16)]
    if is_late:
        scratch += [
            pltpu.VMEM((2, UNIT, tok, GROUP * d), jnp.bfloat16),
            pltpu.VMEM((2, tok, d), jnp.float32),
            pltpu.VMEM((2, total * tok, 2 * d), jnp.bfloat16),
            pltpu.SemaphoreType.DMA((2, UNIT)),
        ]
    mine = {array for _, array in (late if is_late else early)}
    return pl.pallas_call(
        functools.partial(kernel, form),
        out_shape=outs,
        in_specs=[pl.BlockSpec(memory_space=pltpu.SMEM)] + [here] * (1 + len(state))
        + [here if i in mine else anywhere for i in range(len(arrays))],
        out_specs=[anywhere if is_late else here] * len(outs),
        scratch_shapes=scratch,
        compiler_params=pltpu.CompilerParams(vmem_limit_bytes=(28 if total <= 16 else 60) * 1024 * 1024),
        cost_estimate=pl.CostEstimate(flops=COST * q.size, bytes_accessed=q.size, transcendentals=0),
    )(info, q, *state, *arrays)


def join(key, value):
    first = lax.broadcasted_iota(jnp.int32, (2, 1, 1), 0) == 0
    return jnp.where(first, key, value)


class Route:
    def __init__(self, devices):
        self.plane = math.isqrt(devices)
        self.cols = self.plane // 2
        self.levels = devices // self.plane
        self.reach = devices // 2 // self.plane

    def at(self, z, x, c):
        return z * self.plane + x * 2 + c

    def everyone(self, level, cores=(0, 1)):
        return [(z, x, c) for z in range(level, self.levels) for x in range(self.cols) for c in cores]

    def wanted(self, level, src, dst):
        return src < dst if level == 0 else src > dst if level == self.reach else True

    def up(self, level):
        return [(self.at(z - 1, x, c), self.at(z, x, c)) for z, x, c in self.everyone(level)]

    def across(self, level, dx, cores=(0, 1)):
        return [(self.at(z, (x - dx) % self.cols, c), self.at(z, x, c)) for z, x, c in self.everyone(level, cores)
                if self.wanted(level, (x - dx) % self.cols, x)]

    def climb(self, dx, cores):
        return [(self.at(z - 1, x, c), self.at(z, x, c)) for z, x, c in self.everyone(self.reach, cores)
                if self.wanted(self.reach, (x - dx) % self.cols, x)]

    def over(self, level, dx, cores=(0, 1)):
        return [(self.at(z, x, 1 - c), self.at(z, x, c)) for z, x, c in self.everyone(level, cores)
                if (self.wanted(level, 1 - c, c) if dx == 0 else self.wanted(level, (x - dx) % self.cols, x))]

    def carry(self, block, core, attend_early):
        send = lambda array, pairs: lax.ppermute(array, "head", pairs)
        reach, columns = self.reach, range(1, self.cols)
        got = {(0, 0, 0): block}

        def swap(level, dx):
            got[level, dx, 1] = send(got[level, dx, 0], self.over(level, dx))

        def tie(names, *more):
            arrays, more = lax.optimization_barrier(([got[name] for name in names], more))
            got.update(zip(names, arrays))
            return more

        state = None
        for level in range(reach):
            got[level + 1, 0, 0] = send(got[level, 0, 0], self.up(level + 1))
            for dx in columns:
                got[level, dx, 0] = send(got[level, 0, 0], self.across(level, dx))
            if level == 0:
                swap(0, 0)
            if level == 1:
                swap(1, 0)
                tie([(0, dx, 0) for dx in columns] + [(0, 0, 1)])
                state = attend_early(got)
                state, = tie([(0, dx, 0) for dx in columns] + [(1, dx, 0) for dx in columns] + [(2, 0, 0)], state)
            elif level:
                tie([(level, dx, 0) for dx in columns] + [(level + 1, 0, 0)])
        for dx in columns:
            pairs = self.across(reach, dx, (0,)) + self.climb(dx, (1,))
            got[reach, dx, 0] = send(jnp.where(core == 0, got[reach, 0, 0], got[reach - 1, dx, 0]), pairs)
        for level in range(2, reach + 1):
            swap(level, 0)
        for dx in columns:
            for level in range(reach + 1):
                swap(level, dx)
        return got, state

    def order(self):
        names = [(level, dx, other) for dx in range(self.cols) for level in range(self.reach + 1) for other in range(2)]
        early = [n for n in names if n[1] == 0 and n[0] < 2]
        late = [n for n in names if n not in early]
        partial = lambda n: n[1] > 0 and n[0] in (0, self.reach)
        return sorted(early, key=partial), sorted(late, key=partial)

    def block(self, name, me):
        level, dx, other = name
        z, x, c = me // self.plane, me % self.plane // 2, me % 2
        col = (x - dx + self.cols) % self.cols
        core = 1 - c if other else c
        want = self.wanted(level, core, c) if dx == 0 else self.wanted(level, col, x)
        held = (z >= level) & (want | (dx == 0 and other == 0))
        return jnp.where(held, self.at(z - level, col, core), -1)


def local(query, key, value, lengths):
    tok = query.shape[1]
    docs = lengths.shape[1]
    d = HEAD_DIM
    me = lax.axis_index("head")
    route = Route(lax.axis_size("head"))
    early, late = route.order()
    total = len(early) + len(late)
    base = [jnp.where(b >= 0, b * tok, FAR) for b in (route.block(name, me) for name in early + late)]
    info = jnp.stack(base + [me * tok, me % route.plane // 2])
    info = jnp.concatenate([info, lengths[0]]).astype(jnp.int32)

    q = query[0]
    def forms(part):
        if route.cols != 2:
            return None
        lacking = (0, route.reach)
        return [[n for n, name in enumerate(part) if name[1] == 0 or name[0] != lacking[x]] for x in range(2)]

    def listed(got, names, at):
        return [got[name] for name in names], [(at + n, n) for n in range(len(names))]

    def attend_early(got):
        arrays, slots = listed(got, early, 0)
        return attend((total, slots, [], forms(early), docs, tok, rows, len(arrays), False), q, [], arrays, info,
                      [jax.ShapeDtypeStruct(q.shape, jnp.float32),
                       jax.ShapeDtypeStruct((KV_HEADS, tok, d), jnp.float32)])

    rows = 512 if total <= 16 else 128
    got, state = route.carry(join(key, value), me % 2, attend_early)
    arrays, slots = listed(got, early + late, 0)
    first, last = slots[:len(early)], slots[len(early):]
    out, = attend((total, first, last, forms(late), docs, tok, rows, len(arrays), True), q, state, arrays, info,
                  [jax.ShapeDtypeStruct(q.shape, jnp.bfloat16)])
    return out[None]


def solution(mesh):
    placed = (
        P("rep", "head", None),
        P("rep", "head", None),
        P("rep", "head", None),
        P("rep", None),
    )
    return jax.shard_map(
        local, mesh=mesh, in_specs=placed, out_specs=P("rep", "head", None), check_vma=False
    )
```

time: 113 us -> 109 us (0.965)
  starting transfers between devices: 31.7 us -> 29 us
  local copies, waits for them, and re-layouts: 4.27 us -> 2.33 us
  other arithmetic: 0 us -> 1.21 us
    ppermute x13 -> x11, starting transfers between devices: 31.7 us -> 29 us  [carry(): send = lambda array, pairs: lax.ppermute(array, 'head', pairs)]
    select_n x0 -> x2, other arithmetic: none -> 1.2 us  [the longest x1 1.15 us: join(): return jnp.where(first, key, value)]
    unnamed x3 -> x2, local copies, waits for them, and re-layouts: 2.55 us -> 1.59 us
    ppermute x13 -> x11, waiting for transfers between devices: 14.4 us -> 14.5 us  [carry(): send = lambda array, pairs: lax.ppermute(array, 'head', pairs)]
  transfers between devices with their start and end apart: 13 -> 11, of which waited for: 5 -> 5; matrix products, arithmetic and copies ran while one was open for 1% -> 1% of each run, Pallas kernels for 8% -> 5%
where the time goes in v2:
time: 109 us
  Pallas kernels  61.2 us (56%)
  starting transfers between devices  29 us (27%)
  waiting for transfers between devices  14.5 us (13%)
  local copies, waits for them, and re-layouts  2.33 us (2%)
  other arithmetic  1.21 us (1%)
    pallas_call x2, Pallas kernels, attend(): pl.pallas_call(functools.partial(kernel, form), out_shape=outs, in_specs=...  61.2 us
    ppermute x11, starting transfers between devices, carry(): send = lambda array, pairs: lax.ppermute(array, 'head', pairs)  29 us
    ppermute x11, waiting for transfers between devices, carry(): send = lambda array, pairs: lax.ppermute(array, 'head', pairs)  14.5 us
  transfers between devices with their start and end apart: 11, of which 5 were waited for; matrix products, arithmetic and copies ran while one was open for 1% of the time, Pallas kernels for 5%

profile of v2, /device:TPU:17, one launch (start us, length us, event | category | flops | bytes accessed | tf_op | source)
XLA Modules:
  0.0 108.7 jit_solution(8518874552851743569)
XLA Ops:
  0.0 1.1 %broadcast_select_fusion.refs_1_.refs_3_ = bf16[2,128,1024]{2,1,0:T(8,128)(2,1)S(1)} fusion(pred[2]{0:T(512)(128)(4,1)S(1)} %iota_compare_fusion, bf16[128,1024]{1,0:T(8,128)(2,1)} %bitcast.21, bf16[128,1024]{1,0:T(8,128)(2,1)} %bitcast.22), kind=kLoop, calls=%fused_computation | loop fusion | flops 262144 | bytes 1048578 | tf_op jit(solution)/shard_map/jit(_where)/select_n | solution.py:203
  1.2 3.2 %collective-permute-start.2 = (bf16[2,128,1024]{2,1,0:T(8,128)(2,1)S(1)}, bf16[2,128,1024]{2,1,0:T(8,128)(2,1)S(1)}, u32[]{:S(2)}, u32[]{:S(2)}) collective-permute-start(bf16[2,128,1024]{2,1,0:T(8,128)(2,1)S(1)} %broadcast_select_fusion.refs_1_.refs_3_), channel_id=1, source_target_pairs={{0,4},{1,5},{2,6},{3,7},{4,8},{5,9},{6,10},{7,11},{8,12},{9,13},{1... | collective-permute-start | bytes 1572872 | tf_op jit(solution)/shard_map/ppermute | solution.py:238
  4.4 1.3 %collective-permute-start.1 = (bf16[2,128,1024]{2,1,0:T(8,128)(2,1)S(1)}, bf16[2,128,1024]{2,1,0:T(8,128)(2,1)S(1)}, u32[]{:S(2)}, u32[]{:S(2)}) collective-permute-start(bf16[2,128,1024]{2,1,0:T(8,128)(2,1)S(1)} %broadcast_select_fusion.refs_1_.refs_3_), channel_id=1, source_target_pairs={{0,1},{2,3},{4,5},{6,7},{8,9},{10,11},{12,13},{14,15},{16,17},{18,... | collective-permute-start | bytes 1572872 | tf_op jit(solution)/shard_map/ppermute | solution.py:238
  5.7 3.9 %collective-permute-start = (bf16[2,128,1024]{2,1,0:T(8,128)(2,1)S(1)}, bf16[2,128,1024]{2,1,0:T(8,128)(2,1)}, u32[]{:S(2)}, u32[]{:S(2)}) collective-permute-start(bf16[2,128,1024]{2,1,0:T(8,128)(2,1)S(1)} %broadcast_select_fusion.refs_1_.refs_3_), channel_id=1, source_target_pairs={{0,2},{1,3},{4,6},{5,7},{8,10},{9,11},{12,14},{13,15},{16,18},{17,... | collective-permute-start | bytes 1572872 | tf_op jit(solution)/shard_map/ppermute | solution.py:238
  9.6 6.2 %collective-permute-done.2.refs_3_.refs_5_ = bf16[2,128,1024]{2,1,0:T(8,128)(2,1)S(1)} collective-permute-done((bf16[2,128,1024]{2,1,0:T(8,128)(2,1)S(1)}, bf16[2,128,1024]{2,1,0:T(8,128)(2,1)S(1)}, u32[]{:S(2)}, u32[]{:S(2)}) %collective-permute-start.2) | collective-permute-done | bytes 524320 | tf_op jit(solution)/shard_map/ppermute | solution.py:238
  15.8 3.4 %collective-permute-start.5 = (bf16[2,128,1024]{2,1,0:T(8,128)(2,1)S(1)}, bf16[2,128,1024]{2,1,0:T(8,128)(2,1)S(1)}, u32[]{:S(2)}, u32[]{:S(2)}) collective-permute-start(bf16[2,128,1024]{2,1,0:T(8,128)(2,1)S(1)} %collective-permute-done.2.refs_3_.refs_5_), channel_id=1, source_target_pairs={{5,4},{4,5},{7,6},{6,7},{9,8},{8,9},{11,10},{10,11},{13,12},{12,13... | collective-permute-start | bytes 1572872 | tf_op jit(solution)/shard_map/ppermute | solution.py:238
  19.3 3.2 %collective-permute-start.4 = (bf16[2,128,1024]{2,1,0:T(8,128)(2,1)S(1)}, bf16[2,128,1024]{2,1,0:T(8,128)(2,1)S(1)}, u32[]{:S(2)}, u32[]{:S(2)}) collective-permute-start(bf16[2,128,1024]{2,1,0:T(8,128)(2,1)S(1)} %collective-permute-done.2.refs_3_.refs_5_), channel_id=1, source_target_pairs={{4,8},{5,9},{6,10},{7,11},{8,12},{9,13},{10,14},{11,15},{20,24},{2... | collective-permute-start | bytes 1572872 | tf_op jit(solution)/shard_map/ppermute | solution.py:238
  22.5 3.1 %collective-permute-start.3 = (bf16[2,128,1024]{2,1,0:T(8,128)(2,1)S(1)}, bf16[2,128,1024]{2,1,0:T(8,128)(2,1)S(1)}, u32[]{:S(2)}, u32[]{:S(2)}) collective-permute-start(bf16[2,128,1024]{2,1,0:T(8,128)(2,1)S(1)} %collective-permute-done.2.refs_3_.refs_5_), channel_id=1, source_target_pairs={{6,4},{7,5},{4,6},{5,7},{10,8},{11,9},{8,10},{9,11},{14,12},{15,13... | collective-permute-start | bytes 1572872 | tf_op jit(solution)/shard_map/ppermute | solution.py:238
  25.8 0.7 concatenate.3.info
  26.6 0.0 collective-permute-done.1.refs_2_.refs_4_
  26.6 0.0 copy-start
  26.6 1.6 %copy-done = bf16[1,128,8192]{2,1,0:T(8,128)(2,1)S(1)} copy-done((bf16[1,128,8192]{2,1,0:T(8,128)(2,1)S(1)}, bf16[1,128,8192]{2,1,0:T(8,128)(2,1)}, u32[]{:S(2)}) %copy-start) | copy-done | bytes 2097176
  28.2 5.9 %shard_map.46 = (f32[128,8192]{1,0:T(8,128)S(1)}, f32[8,128,128]{2,1,0:T(8,128)S(1)}) custom-call(s32[22]{0:T(128)S(1)} %concatenate.3.info, bf16[128,8192]{1,0:T(8,128)(2,1)S(1)} %bitcast.19, bf16[2,128,1024]{2,1,0:T(8,128)(2,1)S(1)} %broadcast_select_fusion.refs_1_.refs_3_, bf16[2,128,1024]{2,1,0:T(8,128)(2,1)S(1)} %collective-permute-done.1.refs_2_.refs_4_, ...), custom_call_target="tpu_custom_call" | custom-call | flops 16777216 | bytes 1048576 | tf_op jit(solution)/shard_map/pallas_call | solution.py:189
  34.1 0.6 collective-permute-done.4.refs_7_
  34.7 2.9 %collective-permute-done.3.refs_9_ = bf16[2,128,1024]{2,1,0:T(8,128)(2,1)S(1)} collective-permute-done((bf16[2,128,1024]{2,1,0:T(8,128)(2,1)S(1)}, bf16[2,128,1024]{2,1,0:T(8,128)(2,1)S(1)}, u32[]{:S(2)}, u32[]{:S(2)}) %collective-permute-start.3) | collective-permute-done | bytes 524320 | tf_op jit(solution)/shard_map/ppermute | solution.py:238
  37.6 0.1 broadcast_select_fusion.1
  37.7 1.9 %collective-permute-start.9 = (bf16[2,128,1024]{2,1,0:T(8,128)(2,1)S(1)}, bf16[2,128,1024]{2,1,0:T(8,128)(2,1)S(1)}, u32[]{:S(2)}, u32[]{:S(2)}) collective-permute-start(bf16[2,128,1024]{2,1,0:T(8,128)(2,1)S(1)} %broadcast_select_fusion.1), channel_id=1, source_target_pairs={{10,8},{14,12},{5,9},{9,13},{26,24},{30,28},{21,25},{25,29}} | collective-permute-start | bytes 1572872 | tf_op jit(solution)/shard_map/ppermute | solution.py:238
  39.6 2.4 %collective-permute-start.6 = (bf16[2,128,1024]{2,1,0:T(8,128)(2,1)S(1)}, bf16[2,128,1024]{2,1,0:T(8,128)(2,1)S(1)}, u32[]{:S(2)}, u32[]{:S(2)}) collective-permute-start(bf16[2,128,1024]{2,1,0:T(8,128)(2,1)S(1)} %collective-permute-done.4.refs_7_), channel_id=1, source_target_pairs={{9,8},{11,10},{13,12},{15,14},{25,24},{27,26},{29,28},{31,30}} | collective-permute-start | bytes 1572872 | tf_op jit(solution)/shard_map/ppermute | solution.py:238
  42.0 0.7 collective-permute-start.8
  42.7 1.9 %collective-permute-start.7 = (bf16[2,128,1024]{2,1,0:T(8,128)(2,1)S(1)}, bf16[2,128,1024]{2,1,0:T(8,128)(2,1)S(1)}, u32[]{:S(2)}, u32[]{:S(2)}) collective-permute-start(bf16[2,128,1024]{2,1,0:T(8,128)(2,1)S(1)} %collective-permute-done.3.refs_9_), channel_id=1, source_target_pairs={{5,4},{4,5},{7,6},{6,7},{9,8},{8,9},{11,10},{10,11},{13,12},{12,13... | collective-permute-start | bytes 1572872 | tf_op jit(solution)/shard_map/ppermute | solution.py:238
  44.7 3.2 %collective-permute-done.9.refs_13_ = bf16[2,128,1024]{2,1,0:T(8,128)(2,1)S(1)} collective-permute-done((bf16[2,128,1024]{2,1,0:T(8,128)(2,1)S(1)}, bf16[2,128,1024]{2,1,0:T(8,128)(2,1)S(1)}, u32[]{:S(2)}, u32[]{:S(2)}) %collective-permute-start.9) | collective-permute-done | bytes 524320 | tf_op jit(solution)/shard_map/ppermute | solution.py:238
  47.9 3.9 %collective-permute-start.10 = (bf16[2,128,1024]{2,1,0:T(8,128)(2,1)S(1)}, bf16[2,128,1024]{2,1,0:T(8,128)(2,1)S(1)}, u32[]{:S(2)}, u32[]{:S(2)}) collective-permute-start(bf16[2,128,1024]{2,1,0:T(8,128)(2,1)S(1)} %collective-permute-done.9.refs_13_), channel_id=1, source_target_pairs={{9,8},{8,9},{13,12},{12,13},{25,24},{24,25},{29,28},{28,29}} | collective-permute-start | bytes 1572872 | tf_op jit(solution)/shard_map/ppermute | solution.py:238
  51.8 1.5 %collective-permute-done.10.refs_14_ = bf16[2,128,1024]{2,1,0:T(8,128)(2,1)S(1)} collective-permute-done((bf16[2,128,1024]{2,1,0:T(8,128)(2,1)S(1)}, bf16[2,128,1024]{2,1,0:T(8,128)(2,1)S(1)}, u32[]{:S(2)}, u32[]{:S(2)}) %collective-permute-start.10) | collective-permute-done | bytes 524320 | tf_op jit(solution)/shard_map/ppermute | solution.py:238
  53.3 55.3 %shard_map.47 = bf16[128,8192]{1,0:T(8,128)(2,1)} custom-call(s32[22]{0:T(128)S(1)} %concatenate.3.info, bf16[128,8192]{1,0:T(8,128)(2,1)S(1)} %bitcast.20, f32[128,8192]{1,0:T(8,128)S(1)} %get-tuple-element.18.refs_1_, f32[8,128,128]{2,1,0:T(8,128)S(1)} %get-tuple-element.19.refs_2_, bf16[2,128,1024]{2,1,0:T(8,128)(2,1)S(1)} %broadcast_select_fusion.refs_1_.refs_3_, ...), custom_call_target="tpu_custom_call" | custom-call | flops 16777216 | bytes 1048576 | tf_op jit(solution)/shard_map/pallas_call | solution.py:189
  (6 shorter events, 0.0 us)
Async XLA Ops:
  1.2 14.7 %collective-permute-start.2 = (bf16[2,128,1024]{2,1,0:T(8,128)(2,1)S(1)}, bf16[2,128,1024]{2,1,0:T(8,128)(2,1)S(1)}, u32[]{:S(2)}, u32[]{:S(2)}) collective-permute-start(bf16[2,128,1024]{2,1,0:T(8,128)(2,1)S(1)} %broadcast_select_fusion.refs_1_.refs_3_), channel_id=1, source_target_pairs={{0,4},{1,5},{2,6},{3,7},{4,8},{5,9},{6,10},{7,11},{8,12},{9,13},{1... | collective-permute-start | bytes 1572872 | tf_op jit(solution)/shard_map/ppermute | solution.py:238
  4.4 22.2 %collective-permute-start.1 = (bf16[2,128,1024]{2,1,0:T(8,128)(2,1)S(1)}, bf16[2,128,1024]{2,1,0:T(8,128)(2,1)S(1)}, u32[]{:S(2)}, u32[]{:S(2)}) collective-permute-start(bf16[2,128,1024]{2,1,0:T(8,128)(2,1)S(1)} %broadcast_select_fusion.refs_1_.refs_3_), channel_id=1, source_target_pairs={{0,1},{2,3},{4,5},{6,7},{8,9},{10,11},{12,13},{14,15},{16,17},{18,... | collective-permute-start | bytes 1572872 | tf_op jit(solution)/shard_map/ppermute | solution.py:238
  5.7 20.9 %collective-permute-start = (bf16[2,128,1024]{2,1,0:T(8,128)(2,1)S(1)}, bf16[2,128,1024]{2,1,0:T(8,128)(2,1)}, u32[]{:S(2)}, u32[]{:S(2)}) collective-permute-start(bf16[2,128,1024]{2,1,0:T(8,128)(2,1)S(1)} %broadcast_select_fusion.refs_1_.refs_3_), channel_id=1, source_target_pairs={{0,2},{1,3},{4,6},{5,7},{8,10},{9,11},{12,14},{13,15},{16,18},{17,... | collective-permute-start | bytes 1572872 | tf_op jit(solution)/shard_map/ppermute | solution.py:238
  15.8 10.7 %collective-permute-start.5 = (bf16[2,128,1024]{2,1,0:T(8,128)(2,1)S(1)}, bf16[2,128,1024]{2,1,0:T(8,128)(2,1)S(1)}, u32[]{:S(2)}, u32[]{:S(2)}) collective-permute-start(bf16[2,128,1024]{2,1,0:T(8,128)(2,1)S(1)} %collective-permute-done.2.refs_3_.refs_5_), channel_id=1, source_target_pairs={{5,4},{4,5},{7,6},{6,7},{9,8},{8,9},{11,10},{10,11},{13,12},{12,13... | collective-permute-start | bytes 1572872 | tf_op jit(solution)/shard_map/ppermute | solution.py:238
  19.3 15.4 %collective-permute-start.4 = (bf16[2,128,1024]{2,1,0:T(8,128)(2,1)S(1)}, bf16[2,128,1024]{2,1,0:T(8,128)(2,1)S(1)}, u32[]{:S(2)}, u32[]{:S(2)}) collective-permute-start(bf16[2,128,1024]{2,1,0:T(8,128)(2,1)S(1)} %collective-permute-done.2.refs_3_.refs_5_), channel_id=1, source_target_pairs={{4,8},{5,9},{6,10},{7,11},{8,12},{9,13},{10,14},{11,15},{20,24},{2... | collective-permute-start | bytes 1572872 | tf_op jit(solution)/shard_map/ppermute | solution.py:238
  22.5 15.1 %collective-permute-start.3 = (bf16[2,128,1024]{2,1,0:T(8,128)(2,1)S(1)}, bf16[2,128,1024]{2,1,0:T(8,128)(2,1)S(1)}, u32[]{:S(2)}, u32[]{:S(2)}) collective-permute-start(bf16[2,128,1024]{2,1,0:T(8,128)(2,1)S(1)} %collective-permute-done.2.refs_3_.refs_5_), channel_id=1, source_target_pairs={{6,4},{7,5},{4,6},{5,7},{10,8},{11,9},{8,10},{9,11},{14,12},{15,13... | collective-permute-start | bytes 1572872 | tf_op jit(solution)/shard_map/ppermute | solution.py:238
  26.6 1.6 %copy-start = (bf16[1,128,8192]{2,1,0:T(8,128)(2,1)S(1)}, bf16[1,128,8192]{2,1,0:T(8,128)(2,1)}, u32[]{:S(2)}) copy-start(bf16[1,128,8192]{2,1,0:T(8,128)(2,1)} %param.4) | copy-start | bytes 6291460
  37.7 10.2 %collective-permute-start.9 = (bf16[2,128,1024]{2,1,0:T(8,128)(2,1)S(1)}, bf16[2,128,1024]{2,1,0:T(8,128)(2,1)S(1)}, u32[]{:S(2)}, u32[]{:S(2)}) collective-permute-start(bf16[2,128,1024]{2,1,0:T(8,128)(2,1)S(1)} %broadcast_select_fusion.1), channel_id=1, source_target_pairs={{10,8},{14,12},{5,9},{9,13},{26,24},{30,28},{21,25},{25,29}} | collective-permute-start | bytes 1572872 | tf_op jit(solution)/shard_map/ppermute | solution.py:238
  39.6 12.2 %collective-permute-start.6 = (bf16[2,128,1024]{2,1,0:T(8,128)(2,1)S(1)}, bf16[2,128,1024]{2,1,0:T(8,128)(2,1)S(1)}, u32[]{:S(2)}, u32[]{:S(2)}) collective-permute-start(bf16[2,128,1024]{2,1,0:T(8,128)(2,1)S(1)} %collective-permute-done.4.refs_7_), channel_id=1, source_target_pairs={{9,8},{11,10},{13,12},{15,14},{25,24},{27,26},{29,28},{31,30}} | collective-permute-start | bytes 1572872 | tf_op jit(solution)/shard_map/ppermute | solution.py:238
  42.0 9.7 %collective-permute-start.8 = (bf16[2,128,1024]{2,1,0:T(8,128)(2,1)}, bf16[2,128,1024]{2,1,0:T(8,128)(2,1)S(1)}, u32[]{:S(2)}, u32[]{:S(2)}) collective-permute-start(bf16[2,128,1024]{2,1,0:T(8,128)(2,1)} %collective-permute-done.refs_11_), channel_id=1, source_target_pairs={{3,2},{2,3},{7,6},{6,7},{11,10},{10,11},{15,14},{14,15},{19,18},{1... | collective-permute-start | bytes 1572872 | tf_op jit(solution)/shard_map/ppermute | solution.py:238
  42.7 9.1 %collective-permute-start.7 = (bf16[2,128,1024]{2,1,0:T(8,128)(2,1)S(1)}, bf16[2,128,1024]{2,1,0:T(8,128)(2,1)S(1)}, u32[]{:S(2)}, u32[]{:S(2)}) collective-permute-start(bf16[2,128,1024]{2,1,0:T(8,128)(2,1)S(1)} %collective-permute-done.3.refs_9_), channel_id=1, source_target_pairs={{5,4},{4,5},{7,6},{6,7},{9,8},{8,9},{11,10},{10,11},{13,12},{12,13... | collective-permute-start | bytes 1572872 | tf_op jit(solution)/shard_map/ppermute | solution.py:238
  47.9 5.4 %collective-permute-start.10 = (bf16[2,128,1024]{2,1,0:T(8,128)(2,1)S(1)}, bf16[2,128,1024]{2,1,0:T(8,128)(2,1)S(1)}, u32[]{:S(2)}, u32[]{:S(2)}) collective-permute-start(bf16[2,128,1024]{2,1,0:T(8,128)(2,1)S(1)} %collective-permute-done.9.refs_13_), channel_id=1, source_target_pairs={{9,8},{8,9},{13,12},{12,13},{25,24},{24,25},{29,28},{28,29}} | collective-permute-start | bytes 1572872 | tf_op jit(solution)/shard_map/ppermute | solution.py:238

commit v3 on v2

--- a/solution.py
+++ b/solution.py
@@ -40,15 +40,14 @@
 
 
 def kernel(form, info, *refs):
-    total, early, late, cut, docs, tok, rows, count, is_late = form
+    total, before, slots, cut, docs, tok, rows, count, has_state, is_last = form
     d = HEAD_DIM
     wide = GROUP * d
     refs = list(refs)
     q_ref = refs.pop(0)
-    state = [refs.pop(0), refs.pop(0)] if is_late else []
+    state = [refs.pop(0), refs.pop(0)] if has_state else []
     kv_refs, refs = refs[:count], refs[count:]
-    slots = late if is_late else early
-    if is_late:
+    if is_last:
         out_ref, mask_ref, out_buf, limits, everything, sems = refs
     else:
         acc_ref, sum_ref, mask_ref = refs
@@ -94,45 +93,46 @@
             for n in range(rows // tok):
                 j = first // tok + n
                 acc, row_sum = o[n * tok:(n + 1) * tok, :d], o[n * tok:(n + 1) * tok, d:]
-                if is_late:
+                if has_state:
+                    acc = acc + state[0][:, span(g * GROUP + j, d)]
+                if is_last:
                     row_sum = row_sum + state[1][g, :, j:j + 1]
                     least, most = jnp.minimum(least, row_sum), jnp.maximum(most, row_sum)
                     share = pl.reciprocal(row_sum, approx=True)
                     share = share * (2.0 - row_sum * share)
-                    acc = (acc + state[0][:, span(g * GROUP + j, d)]) * share
-                    out_buf[buf, h, :, j * d:(j + 1) * d] = acc.astype(jnp.bfloat16)
+                    out_buf[buf, h, :, j * d:(j + 1) * d] = (acc * share).astype(jnp.bfloat16)
                 else:
                     packed[h] = jnp.where(lane == j, row_sum, packed[h])
                     acc_ref[:, span(g * GROUP + j, d)] = acc
-        if is_late:
+        if is_last:
             limits[0] = jnp.minimum(limits[0], least)
             limits[1] = jnp.maximum(limits[1], most)
         else:
             for h in range(UNIT):
-                sum_ref[u * UNIT + h] = packed[h]
+                sum_ref[u * UNIT + h] = packed[h] + state[1][u * UNIT + h] if has_state else packed[h]
 
     def run(part):
         units = KV_HEADS // UNIT
         for n, mask in enumerate(masks(part, info, total, docs, tok)):
             mask_ref[n * tok:(n + 1) * tok, :] = mask
-        if is_late:
+        if is_last:
             limits[...] = jnp.ones((2, tok, d), jnp.float32)
 
         def step(u, carry):
             buf = lax.rem(u, 2)
-            if is_late:
+            if is_last:
                 @pl.when(u > 1)
                 def _():
                     for h in range(UNIT):
                         result(u - 2, buf, h).wait()
             attend(part, u, buf)
-            if is_late:
+            if is_last:
                 for h in range(UNIT):
                     result(u, buf, h).start()
             return carry
 
         lax.fori_loop(0, units, step, 0)
-        if is_late:
+        if is_last:
             for u in range(units - 2, units):
                 for h in range(UNIT):
                     result(u, u % 2, h).wait()
@@ -143,17 +143,17 @@
         for column, picked in enumerate(cut):
             pl.when(info[total + 1] == column)(functools.partial(run, [slots[n] for n in picked]))
 
-    if is_late:
+    if is_last:
         inside = (limits[0] >= LOWEST) & (limits[1] <= HIGHEST)
 
         @pl.when(jnp.max(jnp.where(inside, 0.0, 1.0)) > 0.0)
         def _():
-            for n, mask in enumerate(masks(early + late, info, total, docs, tok)):
+            for n, mask in enumerate(masks(before + slots, info, total, docs, tok)):
                 everything[0, n * tok:(n + 1) * tok, d:] = mask
                 everything[1, n * tok:(n + 1) * tok, d:] = one
 
             def again(g, carry):
-                for n, (_, array) in enumerate(early + late):
+                for n, (_, array) in enumerate(before + slots):
                     copy = pltpu.make_async_copy(kv_refs[array].at[:, :, span(g, d)],
                                                  everything.at[:, n * tok:(n + 1) * tok, :d], sems.at[0, 0])
                     copy.start()
@@ -173,27 +173,27 @@
 
 
 def attend(form, q, state, arrays, info, outs):
-    total, early, late, cut, docs, tok, rows, count, is_late = form
+    total, before, slots, cut, docs, tok, rows, count, has_state, is_last = form
     d = HEAD_DIM
-    n = max(len(picked) for picked in cut) if cut else len(late if is_late else early)
+    n = max(len(picked) for picked in cut) if cut else len(slots)
     anywhere, here = pl.BlockSpec(memory_space=pl.ANY), pl.BlockSpec(memory_space=pltpu.VMEM)
     scratch = [pltpu.VMEM((n * tok, d), jnp.bfloat16)]
-    if is_late:
+    if is_last:
         scratch += [
             pltpu.VMEM((2, UNIT, tok, GROUP * d), jnp.bfloat16),
             pltpu.VMEM((2, tok, d), jnp.float32),
             pltpu.VMEM((2, total * tok, 2 * d), jnp.bfloat16),
             pltpu.SemaphoreType.DMA((2, UNIT)),
         ]
-    mine = {array for _, array in (late if is_late else early)}
+    mine = {array for _, array in slots}
     return pl.pallas_call(
         functools.partial(kernel, form),
         out_shape=outs,
         in_specs=[pl.BlockSpec(memory_space=pltpu.SMEM)] + [here] * (1 + len(state))
         + [here if i in mine else anywhere for i in range(len(arrays))],
-        out_specs=[anywhere if is_late else here] * len(outs),
+        out_specs=[anywhere if is_last else here] * len(outs),
         scratch_shapes=scratch,
-        compiler_params=pltpu.CompilerParams(vmem_limit_bytes=(28 if total <= 16 else 60) * 1024 * 1024),
+        compiler_params=pltpu.CompilerParams(vmem_limit_bytes=(16 if total <= 16 else 60) * 1024 * 1024),
         cost_estimate=pl.CostEstimate(flops=COST * q.size, bytes_accessed=q.size, transcendentals=0),
     )(info, q, *state, *arrays)
 
@@ -234,7 +234,7 @@
         return [(self.at(z, x, 1 - c), self.at(z, x, c)) for z, x, c in self.everyone(level, cores)
                 if (self.wanted(level, 1 - c, c) if dx == 0 else self.wanted(level, (x - dx) % self.cols, x))]
 
-    def carry(self, block, core, attend_early):
+    def carry(self, block, core, attend_early, attend_middle):
         send = lambda array, pairs: lax.ppermute(array, "head", pairs)
         reach, columns = self.reach, range(1, self.cols)
         got = {(0, 0, 0): block}
@@ -267,16 +267,18 @@
         for level in range(2, reach + 1):
             swap(level, 0)
         for dx in columns:
-            for level in range(reach + 1):
+            for level in range(reach):
                 swap(level, dx)
+        state, = tie([(reach, dx, 0) for dx in columns], attend_middle(got, state))
+        for dx in columns:
+            swap(reach, dx)
         return got, state
 
     def order(self):
         names = [(level, dx, other) for dx in range(self.cols) for level in range(self.reach + 1) for other in range(2)]
         early = [n for n in names if n[1] == 0 and n[0] < 2]
-        late = [n for n in names if n not in early]
-        partial = lambda n: n[1] > 0 and n[0] in (0, self.reach)
-        return sorted(early, key=partial), sorted(late, key=partial)
+        middle = [n for n in names if n[2] == 0 and (n[0] > 1 if n[1] == 0 else 0 < n[0] < self.reach)]
+        return early, middle, [n for n in names if n not in early + middle]
 
     def block(self, name, me):
         level, dx, other = name
@@ -294,34 +296,35 @@
     d = HEAD_DIM
     me = lax.axis_index("head")
     route = Route(lax.axis_size("head"))
-    early, late = route.order()
-    total = len(early) + len(late)
-    base = [jnp.where(b >= 0, b * tok, FAR) for b in (route.block(name, me) for name in early + late)]
+    parts = route.order()
+    names = sum(parts, [])
+    total = len(names)
+    base = [jnp.where(b >= 0, b * tok, FAR) for b in (route.block(name, me) for name in names)]
     info = jnp.stack(base + [me * tok, me % route.plane // 2])
     info = jnp.concatenate([info, lengths[0]]).astype(jnp.int32)
-
     q = query[0]
+    rows = 512 if total <= 16 else 128
+
     def forms(part):
-        if route.cols != 2:
+        if route.cols != 2 or all(name[1] == 0 or 0 < name[0] < route.reach for name in part):
             return None
         lacking = (0, route.reach)
         return [[n for n, name in enumerate(part) if name[1] == 0 or name[0] != lacking[x]] for x in range(2)]
 
-    def listed(got, names, at):
-        return [got[name] for name in names], [(at + n, n) for n in range(len(names))]
-
-    def attend_early(got):
-        arrays, slots = listed(got, early, 0)
-        return attend((total, slots, [], forms(early), docs, tok, rows, len(arrays), False), q, [], arrays, info,
-                      [jax.ShapeDtypeStruct(q.shape, jnp.float32),
-                       jax.ShapeDtypeStruct((KV_HEADS, tok, d), jnp.float32)])
-
-    rows = 512 if total <= 16 else 128
-    got, state = route.carry(join(key, value), me % 2, attend_early)
-    arrays, slots = listed(got, early + late, 0)
-    first, last = slots[:len(early)], slots[len(early):]
-    out, = attend((total, first, last, forms(late), docs, tok, rows, len(arrays), True), q, state, arrays, info,
-                  [jax.ShapeDtypeStruct(q.shape, jnp.bfloat16)])
+    def work(got, stage, state):
+        first = sum(len(part) for part in parts[:stage])
+        is_last = stage + 1 == len(parts)
+        known = names if is_last else parts[stage]
+        slots = [(first + n, n + (first if is_last else 0)) for n in range(len(parts[stage]))]
+        before = [(n, n) for n in range(first)]
+        outs = [jax.ShapeDtypeStruct(q.shape, jnp.float32), jax.ShapeDtypeStruct((KV_HEADS, tok, d), jnp.float32)]
+        if is_last:
+            outs = [jax.ShapeDtypeStruct(q.shape, jnp.bfloat16)]
+        form = (total, before, slots, forms(parts[stage]), docs, tok, rows, len(known), bool(state), is_last)
+        return attend(form, q, state, [got[name] for name in known], info, outs)
+
+    got, state = route.carry(join(key, value), me % 2, lambda got: work(got, 0, []), lambda got, state: work(got, 1, state))
+    out, = work(got, 2, state)
     return out[None]
 
 

time: 109 us -> 107 us (0.982)
  waiting for transfers between devices: 14.5 us -> 11.2 us
  Pallas kernels: 61.2 us -> 62.6 us
    ppermute x11, waiting for transfers between devices: 14.5 us -> 11.2 us  [carry(): send = lambda array, pairs: lax.ppermute(array, 'head', pairs)]
    pallas_call x2 -> x3, Pallas kernels: 61.2 us -> 62.6 us  [attend(): pl.pallas_call(functools.partial(kernel, form), out_shape=outs, in_specs=...]
  transfers between devices with their start and end apart: 11 -> 11, of which waited for: 5 -> 4; matrix products, arithmetic and copies ran while one was open for 1% -> 1% of each run, Pallas kernels for 5% -> 9%
where the time goes in v3:
time: 107 us; the launch traced here: 106 us
  Pallas kernels  62.6 us (59%)
  starting transfers between devices  28.4 us (27%)
  waiting for transfers between devices  11.2 us (10%)
  local copies, waits for them, and re-layouts  2.33 us (2%)
  other arithmetic  1.21 us (1%)
    pallas_call x3, Pallas kernels, attend(): pl.pallas_call(functools.partial(kernel, form), out_shape=outs, in_specs=...  62.6 us
    ppermute x11, starting transfers between devices, carry(): send = lambda array, pairs: lax.ppermute(array, 'head', pairs)  28.4 us
    ppermute x11, waiting for transfers between devices, carry(): send = lambda array, pairs: lax.ppermute(array, 'head', pairs)  11.2 us
  transfers between devices with their start and end apart: 11, of which 4 were waited for; matrix products, arithmetic and copies ran while one was open for 1% of the time, Pallas kernels for 9%

profile of v3, /device:TPU:17, one launch (start us, length us, event | category | flops | bytes accessed | tf_op | source)
XLA Modules:
  0.0 106.1 jit_solution(13092155809742825873)
XLA Ops:
  0.0 1.1 %broadcast_select_fusion.refs_1_.refs_3_ = bf16[2,128,1024]{2,1,0:T(8,128)(2,1)S(1)} fusion(pred[2]{0:T(512)(128)(4,1)S(1)} %iota_compare_fusion, bf16[128,1024]{1,0:T(8,128)(2,1)} %bitcast.22, bf16[128,1024]{1,0:T(8,128)(2,1)} %bitcast.23), kind=kLoop, calls=%fused_computation | loop fusion | flops 262144 | bytes 1048578 | tf_op jit(solution)/shard_map/jit(_where)/select_n | solution.py:203
  1.2 3.2 %collective-permute-start.2 = (bf16[2,128,1024]{2,1,0:T(8,128)(2,1)S(1)}, bf16[2,128,1024]{2,1,0:T(8,128)(2,1)S(1)}, u32[]{:S(2)}, u32[]{:S(2)}) collective-permute-start(bf16[2,128,1024]{2,1,0:T(8,128)(2,1)S(1)} %broadcast_select_fusion.refs_1_.refs_3_), channel_id=1, source_target_pairs={{0,4},{1,5},{2,6},{3,7},{4,8},{5,9},{6,10},{7,11},{8,12},{9,13},{1... | collective-permute-start | bytes 1572872 | tf_op jit(solution)/shard_map/ppermute | solution.py:238
  4.4 1.3 %collective-permute-start.1 = (bf16[2,128,1024]{2,1,0:T(8,128)(2,1)S(1)}, bf16[2,128,1024]{2,1,0:T(8,128)(2,1)S(1)}, u32[]{:S(2)}, u32[]{:S(2)}) collective-permute-start(bf16[2,128,1024]{2,1,0:T(8,128)(2,1)S(1)} %broadcast_select_fusion.refs_1_.refs_3_), channel_id=1, source_target_pairs={{0,1},{2,3},{4,5},{6,7},{8,9},{10,11},{12,13},{14,15},{16,17},{18,... | collective-permute-start | bytes 1572872 | tf_op jit(solution)/shard_map/ppermute | solution.py:238
  5.7 3.9 %collective-permute-start = (bf16[2,128,1024]{2,1,0:T(8,128)(2,1)S(1)}, bf16[2,128,1024]{2,1,0:T(8,128)(2,1)}, u32[]{:S(2)}, u32[]{:S(2)}) collective-permute-start(bf16[2,128,1024]{2,1,0:T(8,128)(2,1)S(1)} %broadcast_select_fusion.refs_1_.refs_3_), channel_id=1, source_target_pairs={{0,2},{1,3},{4,6},{5,7},{8,10},{9,11},{12,14},{13,15},{16,18},{17,... | collective-permute-start | bytes 1572872 | tf_op jit(solution)/shard_map/ppermute | solution.py:238
  9.6 6.3 %collective-permute-done.2.refs_3_.refs_5_ = bf16[2,128,1024]{2,1,0:T(8,128)(2,1)S(1)} collective-permute-done((bf16[2,128,1024]{2,1,0:T(8,128)(2,1)S(1)}, bf16[2,128,1024]{2,1,0:T(8,128)(2,1)S(1)}, u32[]{:S(2)}, u32[]{:S(2)}) %collective-permute-start.2) | collective-permute-done | bytes 524320 | tf_op jit(solution)/shard_map/ppermute | solution.py:238
  15.8 3.4 %collective-permute-start.5 = (bf16[2,128,1024]{2,1,0:T(8,128)(2,1)S(1)}, bf16[2,128,1024]{2,1,0:T(8,128)(2,1)S(1)}, u32[]{:S(2)}, u32[]{:S(2)}) collective-permute-start(bf16[2,128,1024]{2,1,0:T(8,128)(2,1)S(1)} %collective-permute-done.2.refs_3_.refs_5_), channel_id=1, source_target_pairs={{5,4},{4,5},{7,6},{6,7},{9,8},{8,9},{11,10},{10,11},{13,12},{12,13... | collective-permute-start | bytes 1572872 | tf_op jit(solution)/shard_map/ppermute | solution.py:238
  19.3 3.2 %collective-permute-start.4 = (bf16[2,128,1024]{2,1,0:T(8,128)(2,1)S(1)}, bf16[2,128,1024]{2,1,0:T(8,128)(2,1)S(1)}, u32[]{:S(2)}, u32[]{:S(2)}) collective-permute-start(bf16[2,128,1024]{2,1,0:T(8,128)(2,1)S(1)} %collective-permute-done.2.refs_3_.refs_5_), channel_id=1, source_target_pairs={{4,8},{5,9},{6,10},{7,11},{8,12},{9,13},{10,14},{11,15},{20,24},{2... | collective-permute-start | bytes 1572872 | tf_op jit(solution)/shard_map/ppermute | solution.py:238
  22.5 3.1 %collective-permute-start.3 = (bf16[2,128,1024]{2,1,0:T(8,128)(2,1)S(1)}, bf16[2,128,1024]{2,1,0:T(8,128)(2,1)S(1)}, u32[]{:S(2)}, u32[]{:S(2)}) collective-permute-start(bf16[2,128,1024]{2,1,0:T(8,128)(2,1)S(1)} %collective-permute-done.2.refs_3_.refs_5_), channel_id=1, source_target_pairs={{6,4},{7,5},{4,6},{5,7},{10,8},{11,9},{8,10},{9,11},{14,12},{15,13... | collective-permute-start | bytes 1572872 | tf_op jit(solution)/shard_map/ppermute | solution.py:238
  25.8 0.7 concatenate.3.info
  26.6 0.0 collective-permute-done.refs_10_
  26.6 0.0 copy-start
  26.6 1.6 %copy-done = bf16[1,128,8192]{2,1,0:T(8,128)(2,1)S(1)} copy-done((bf16[1,128,8192]{2,1,0:T(8,128)(2,1)S(1)}, bf16[1,128,8192]{2,1,0:T(8,128)(2,1)}, u32[]{:S(2)}) %copy-start) | copy-done | bytes 2097176
  28.2 5.9 %shard_map.46 = (f32[128,8192]{1,0:T(8,128)S(1)}, f32[8,128,128]{2,1,0:T(8,128)S(1)}) custom-call(s32[22]{0:T(128)S(1)} %concatenate.3.info, bf16[128,8192]{1,0:T(8,128)(2,1)S(1)} %bitcast.19, bf16[2,128,1024]{2,1,0:T(8,128)(2,1)S(1)} %broadcast_select_fusion.refs_1_.refs_3_, bf16[2,128,1024]{2,1,0:T(8,128)(2,1)S(1)} %collective-permute-done.1.refs_2_.refs_4_, ...), custom_call_target="tpu_custom_call" | custom-call | flops 16777216 | bytes 1048576 | tf_op jit(solution)/shard_map/pallas_call | solution.py:189
  34.1 0.6 collective-permute-done.4.refs_3_.refs_7_
  34.7 2.9 %collective-permute-done.3.refs_4_.refs_8_ = bf16[2,128,1024]{2,1,0:T(8,128)(2,1)S(1)} collective-permute-done((bf16[2,128,1024]{2,1,0:T(8,128)(2,1)S(1)}, bf16[2,128,1024]{2,1,0:T(8,128)(2,1)S(1)}, u32[]{:S(2)}, u32[]{:S(2)}) %collective-permute-start.3) | collective-permute-done | bytes 524320 | tf_op jit(solution)/shard_map/ppermute | solution.py:238
  37.6 0.1 broadcast_select_fusion.1
  37.7 1.9 %collective-permute-start.6 = (bf16[2,128,1024]{2,1,0:T(8,128)(2,1)S(1)}, bf16[2,128,1024]{2,1,0:T(8,128)(2,1)S(1)}, u32[]{:S(2)}, u32[]{:S(2)}) collective-permute-start(bf16[2,128,1024]{2,1,0:T(8,128)(2,1)S(1)} %broadcast_select_fusion.1), channel_id=1, source_target_pairs={{10,8},{14,12},{5,9},{9,13},{26,24},{30,28},{21,25},{25,29}} | collective-permute-start | bytes 1572872 | tf_op jit(solution)/shard_map/ppermute | solution.py:238
  39.6 2.4 %collective-permute-start.7 = (bf16[2,128,1024]{2,1,0:T(8,128)(2,1)S(1)}, bf16[2,128,1024]{2,1,0:T(8,128)(2,1)S(1)}, u32[]{:S(2)}, u32[]{:S(2)}) collective-permute-start(bf16[2,128,1024]{2,1,0:T(8,128)(2,1)S(1)} %collective-permute-done.4.refs_3_.refs_7_), channel_id=1, source_target_pairs={{9,8},{11,10},{13,12},{15,14},{25,24},{27,26},{29,28},{31,30}} | collective-permute-start | bytes 1572872 | tf_op jit(solution)/shard_map/ppermute | solution.py:238
  42.0 1.9 %collective-permute-start.9 = (bf16[2,128,1024]{2,1,0:T(8,128)(2,1)S(1)}, bf16[2,128,1024]{2,1,0:T(8,128)(2,1)S(1)}, u32[]{:S(2)}, u32[]{:S(2)}) collective-permute-start(bf16[2,128,1024]{2,1,0:T(8,128)(2,1)S(1)} %collective-permute-done.3.refs_4_.refs_8_), channel_id=1, source_target_pairs={{5,4},{4,5},{7,6},{6,7},{9,8},{8,9},{11,10},{10,11},{13,12},{12,13... | collective-permute-start | bytes 1572872 | tf_op jit(solution)/shard_map/ppermute | solution.py:238
  44.0 0.7 collective-permute-start.8
  44.7 3.9 %shard_map.47 = (f32[128,8192]{1,0:T(8,128)S(1)}, f32[8,128,128]{2,1,0:T(8,128)S(1)}) custom-call(s32[22]{0:T(128)S(1)} %concatenate.3.info, bf16[128,8192]{1,0:T(8,128)(2,1)S(1)} %bitcast.20, f32[128,8192]{1,0:T(8,128)S(1)} %get-tuple-element.25.refs_1_, f32[8,128,128]{2,1,0:T(8,128)S(1)} %get-tuple-element.26.refs_2_, ...), custom_call_target="tpu_custom_call" | custom-call | flops 16777216 | bytes 1048576 | tf_op jit(solution)/shard_map/pallas_call | solution.py:189
  48.6 3.2 %collective-permute-start.10 = (bf16[2,128,1024]{2,1,0:T(8,128)(2,1)S(1)}, bf16[2,128,1024]{2,1,0:T(8,128)(2,1)S(1)}, u32[]{:S(2)}, u32[]{:S(2)}) collective-permute-start(bf16[2,128,1024]{2,1,0:T(8,128)(2,1)S(1)} %collective-permute-done.6.refs_13_), channel_id=1, source_target_pairs={{9,8},{8,9},{13,12},{12,13},{25,24},{24,25},{29,28},{28,29}} | collective-permute-start | bytes 1572872 | tf_op jit(solution)/shard_map/ppermute | solution.py:238
  51.8 1.5 %collective-permute-done.10.refs_14_ = bf16[2,128,1024]{2,1,0:T(8,128)(2,1)S(1)} collective-permute-done((bf16[2,128,1024]{2,1,0:T(8,128)(2,1)S(1)}, bf16[2,128,1024]{2,1,0:T(8,128)(2,1)S(1)}, u32[]{:S(2)}, u32[]{:S(2)}) %collective-permute-start.10) | collective-permute-done | bytes 524320 | tf_op jit(solution)/shard_map/ppermute | solution.py:238
  53.3 52.8 %shard_map.48 = bf16[128,8192]{1,0:T(8,128)(2,1)} custom-call(s32[22]{0:T(128)S(1)} %concatenate.3.info, bf16[128,8192]{1,0:T(8,128)(2,1)S(1)} %bitcast.21, f32[128,8192]{1,0:T(8,128)S(1)} %get-tuple-element.29.refs_1_, f32[8,128,128]{2,1,0:T(8,128)S(1)} %get-tuple-element.30.refs_2_, bf16[2,128,1024]{2,1,0:T(8,128)(2,1)S(1)} %broadcast_select_fusion.refs_1_.refs_3_, ...), custom_call_target="tpu_custom_call" | custom-call | flops 16777216 | bytes 1048576 | tf_op jit(solution)/shard_map/pallas_call | solution.py:189
  (7 shorter events, 0.0 us)
Async XLA Ops:
  1.2 14.7 %collective-permute-start.2 = (bf16[2,128,1024]{2,1,0:T(8,128)(2,1)S(1)}, bf16[2,128,1024]{2,1,0:T(8,128)(2,1)S(1)}, u32[]{:S(2)}, u32[]{:S(2)}) collective-permute-start(bf16[2,128,1024]{2,1,0:T(8,128)(2,1)S(1)} %broadcast_select_fusion.refs_1_.refs_3_), channel_id=1, source_target_pairs={{0,4},{1,5},{2,6},{3,7},{4,8},{5,9},{6,10},{7,11},{8,12},{9,13},{1... | collective-permute-start | bytes 1572872 | tf_op jit(solution)/shard_map/ppermute | solution.py:238
  4.4 22.2 %collective-permute-start.1 = (bf16[2,128,1024]{2,1,0:T(8,128)(2,1)S(1)}, bf16[2,128,1024]{2,1,0:T(8,128)(2,1)S(1)}, u32[]{:S(2)}, u32[]{:S(2)}) collective-permute-start(bf16[2,128,1024]{2,1,0:T(8,128)(2,1)S(1)} %broadcast_select_fusion.refs_1_.refs_3_), channel_id=1, source_target_pairs={{0,1},{2,3},{4,5},{6,7},{8,9},{10,11},{12,13},{14,15},{16,17},{18,... | collective-permute-start | bytes 1572872 | tf_op jit(solution)/shard_map/ppermute | solution.py:238
  5.7 20.9 %collective-permute-start = (bf16[2,128,1024]{2,1,0:T(8,128)(2,1)S(1)}, bf16[2,128,1024]{2,1,0:T(8,128)(2,1)}, u32[]{:S(2)}, u32[]{:S(2)}) collective-permute-start(bf16[2,128,1024]{2,1,0:T(8,128)(2,1)S(1)} %broadcast_select_fusion.refs_1_.refs_3_), channel_id=1, source_target_pairs={{0,2},{1,3},{4,6},{5,7},{8,10},{9,11},{12,14},{13,15},{16,18},{17,... | collective-permute-start | bytes 1572872 | tf_op jit(solution)/shard_map/ppermute | solution.py:238
  15.8 10.7 %collective-permute-start.5 = (bf16[2,128,1024]{2,1,0:T(8,128)(2,1)S(1)}, bf16[2,128,1024]{2,1,0:T(8,128)(2,1)S(1)}, u32[]{:S(2)}, u32[]{:S(2)}) collective-permute-start(bf16[2,128,1024]{2,1,0:T(8,128)(2,1)S(1)} %collective-permute-done.2.refs_3_.refs_5_), channel_id=1, source_target_pairs={{5,4},{4,5},{7,6},{6,7},{9,8},{8,9},{11,10},{10,11},{13,12},{12,13... | collective-permute-start | bytes 1572872 | tf_op jit(solution)/shard_map/ppermute | solution.py:238
  19.3 15.4 %collective-permute-start.4 = (bf16[2,128,1024]{2,1,0:T(8,128)(2,1)S(1)}, bf16[2,128,1024]{2,1,0:T(8,128)(2,1)S(1)}, u32[]{:S(2)}, u32[]{:S(2)}) collective-permute-start(bf16[2,128,1024]{2,1,0:T(8,128)(2,1)S(1)} %collective-permute-done.2.refs_3_.refs_5_), channel_id=1, source_target_pairs={{4,8},{5,9},{6,10},{7,11},{8,12},{9,13},{10,14},{11,15},{20,24},{2... | collective-permute-start | bytes 1572872 | tf_op jit(solution)/shard_map/ppermute | solution.py:238
  22.5 15.1 %collective-permute-start.3 = (bf16[2,128,1024]{2,1,0:T(8,128)(2,1)S(1)}, bf16[2,128,1024]{2,1,0:T(8,128)(2,1)S(1)}, u32[]{:S(2)}, u32[]{:S(2)}) collective-permute-start(bf16[2,128,1024]{2,1,0:T(8,128)(2,1)S(1)} %collective-permute-done.2.refs_3_.refs_5_), channel_id=1, source_target_pairs={{6,4},{7,5},{4,6},{5,7},{10,8},{11,9},{8,10},{9,11},{14,12},{15,13... | collective-permute-start | bytes 1572872 | tf_op jit(solution)/shard_map/ppermute | solution.py:238
  26.6 1.6 %copy-start = (bf16[1,128,8192]{2,1,0:T(8,128)(2,1)S(1)}, bf16[1,128,8192]{2,1,0:T(8,128)(2,1)}, u32[]{:S(2)}) copy-start(bf16[1,128,8192]{2,1,0:T(8,128)(2,1)} %param.4) | copy-start | bytes 6291460
  37.7 10.9 %collective-permute-start.6 = (bf16[2,128,1024]{2,1,0:T(8,128)(2,1)S(1)}, bf16[2,128,1024]{2,1,0:T(8,128)(2,1)S(1)}, u32[]{:S(2)}, u32[]{:S(2)}) collective-permute-start(bf16[2,128,1024]{2,1,0:T(8,128)(2,1)S(1)} %broadcast_select_fusion.1), channel_id=1, source_target_pairs={{10,8},{14,12},{5,9},{9,13},{26,24},{30,28},{21,25},{25,29}} | collective-permute-start | bytes 1572872 | tf_op jit(solution)/shard_map/ppermute | solution.py:238
  39.6 12.2 %collective-permute-start.7 = (bf16[2,128,1024]{2,1,0:T(8,128)(2,1)S(1)}, bf16[2,128,1024]{2,1,0:T(8,128)(2,1)S(1)}, u32[]{:S(2)}, u32[]{:S(2)}) collective-permute-start(bf16[2,128,1024]{2,1,0:T(8,128)(2,1)S(1)} %collective-permute-done.4.refs_3_.refs_7_), channel_id=1, source_target_pairs={{9,8},{11,10},{13,12},{15,14},{25,24},{27,26},{29,28},{31,30}} | collective-permute-start | bytes 1572872 | tf_op jit(solution)/shard_map/ppermute | solution.py:238
  42.0 9.8 %collective-permute-start.9 = (bf16[2,128,1024]{2,1,0:T(8,128)(2,1)S(1)}, bf16[2,128,1024]{2,1,0:T(8,128)(2,1)S(1)}, u32[]{:S(2)}, u32[]{:S(2)}) collective-permute-start(bf16[2,128,1024]{2,1,0:T(8,128)(2,1)S(1)} %collective-permute-done.3.refs_4_.refs_8_), channel_id=1, source_target_pairs={{5,4},{4,5},{7,6},{6,7},{9,8},{8,9},{11,10},{10,11},{13,12},{12,13... | collective-permute-start | bytes 1572872 | tf_op jit(solution)/shard_map/ppermute | solution.py:238
  44.0 7.8 %collective-permute-start.8 = (bf16[2,128,1024]{2,1,0:T(8,128)(2,1)}, bf16[2,128,1024]{2,1,0:T(8,128)(2,1)S(1)}, u32[]{:S(2)}, u32[]{:S(2)}) collective-permute-start(bf16[2,128,1024]{2,1,0:T(8,128)(2,1)} %collective-permute-done.refs_10_), channel_id=1, source_target_pairs={{3,2},{2,3},{7,6},{6,7},{11,10},{10,11},{15,14},{14,15},{19,18},{1... | collective-permute-start | bytes 1572872 | tf_op jit(solution)/shard_map/ppermute | solution.py:238
  48.6 4.7 %collective-permute-start.10 = (bf16[2,128,1024]{2,1,0:T(8,128)(2,1)S(1)}, bf16[2,128,1024]{2,1,0:T(8,128)(2,1)S(1)}, u32[]{:S(2)}, u32[]{:S(2)}) collective-permute-start(bf16[2,128,1024]{2,1,0:T(8,128)(2,1)S(1)} %collective-permute-done.6.refs_13_), channel_id=1, source_target_pairs={{9,8},{8,9},{13,12},{12,13},{25,24},{24,25},{29,28},{28,29}} | collective-permute-start | bytes 1572872 | tf_op jit(solution)/shard_map/ppermute | solution.py:238

commit v4 on v3

--- a/solution.py
+++ b/solution.py
@@ -15,7 +15,7 @@
 BIG = -1e30
 FAR = 1 << 29
 SCALE = float(HEAD_DIM) ** -0.5 * math.log2(math.e)
-UNIT = 2
+UNIT = 4
 TILE = 256
 LOWEST, HIGHEST = 2.0 ** -40, 2.0 ** 100
 COST = 16
@@ -104,6 +104,8 @@
                 else:
                     packed[h] = jnp.where(lane == j, row_sum, packed[h])
                     acc_ref[:, span(g * GROUP + j, d)] = acc
+            if is_last and first + rows == GROUP * tok:
+                result(u, buf, h).start()
         if is_last:
             limits[0] = jnp.minimum(limits[0], least)
             limits[1] = jnp.maximum(limits[1], most)
@@ -126,9 +128,6 @@
                     for h in range(UNIT):
                         result(u - 2, buf, h).wait()
             attend(part, u, buf)
-            if is_last:
-                for h in range(UNIT):
-                    result(u, buf, h).start()
             return carry
 
         lax.fori_loop(0, units, step, 0)
@@ -276,9 +275,9 @@
 
     def order(self):
         names = [(level, dx, other) for dx in range(self.cols) for level in range(self.reach + 1) for other in range(2)]
-        early = [n for n in names if n[1] == 0 and n[0] < 2]
-        middle = [n for n in names if n[2] == 0 and (n[0] > 1 if n[1] == 0 else 0 < n[0] < self.reach)]
-        return early, middle, [n for n in names if n not in early + middle]
+        early = [n for n in names if n[0] == 0 and 0 in n[1:] or n == (1, 0, 0)]
+        last = [n for n in names if n[1] > 0 and (n[0] == self.reach or n[2] == 1) or n[0] > 1 and n[2] == 1]
+        return early, [n for n in names if n not in early + last], last
 
     def block(self, name, me):
         level, dx, other = name

time: 107 us -> 103 us (0.963)
  waiting for transfers between devices: 11.2 us -> 8.52 us
  starting transfers between devices: 28.4 us -> 27.3 us
    ppermute x11, waiting for transfers between devices: 11.2 us -> 8.52 us  [carry(): send = lambda array, pairs: lax.ppermute(array, 'head', pairs)]
  transfers between devices with their start and end apart: 11 -> 11, of which waited for: 4 -> 2; matrix products, arithmetic and copies ran while one was open for 1% -> 1% of each run, Pallas kernels for 9% -> 11%
where the time goes in v4:
time: 103 us
  Pallas kernels  62.9 us (61%)
  starting transfers between devices  27.3 us (27%)
  waiting for transfers between devices  8.52 us (8%)
  local copies, waits for them, and re-layouts  2.33 us (2%)
  other arithmetic  1.21 us (1%)
    pallas_call x3, Pallas kernels, attend(): pl.pallas_call(functools.partial(kernel, form), out_shape=outs, in_specs=...  62.9 us
    ppermute x11, starting transfers between devices, carry(): send = lambda array, pairs: lax.ppermute(array, 'head', pairs)  27.3 us
    ppermute x11, waiting for transfers between devices, carry(): send = lambda array, pairs: lax.ppermute(array, 'head', pairs)  8.52 us
  transfers between devices with their start and end apart: 11, of which 2 were waited for; matrix products, arithmetic and copies ran while one was open for 1% of the time, Pallas kernels for 11%

profile of v4, /device:TPU:17, one launch (start us, length us, event | category | flops | bytes accessed | tf_op | source)
XLA Modules:
  0.0 102.8 jit_solution(9253945692948727556)
XLA Ops:
  0.0 1.1 %broadcast_select_fusion.refs_1_.refs_3_ = bf16[2,128,1024]{2,1,0:T(8,128)(2,1)S(1)} fusion(pred[2]{0:T(512)(128)(4,1)S(1)} %iota_compare_fusion, bf16[128,1024]{1,0:T(8,128)(2,1)} %bitcast.22, bf16[128,1024]{1,0:T(8,128)(2,1)} %bitcast.23), kind=kLoop, calls=%fused_computation | loop fusion | flops 262144 | bytes 1048578 | tf_op jit(solution)/shard_map/jit(_where)/select_n | solution.py:202
  1.2 3.2 %collective-permute-start.2 = (bf16[2,128,1024]{2,1,0:T(8,128)(2,1)S(1)}, bf16[2,128,1024]{2,1,0:T(8,128)(2,1)S(1)}, u32[]{:S(2)}, u32[]{:S(2)}) collective-permute-start(bf16[2,128,1024]{2,1,0:T(8,128)(2,1)S(1)} %broadcast_select_fusion.refs_1_.refs_3_), channel_id=1, source_target_pairs={{0,4},{1,5},{2,6},{3,7},{4,8},{5,9},{6,10},{7,11},{8,12},{9,13},{1... | collective-permute-start | bytes 1572872 | tf_op jit(solution)/shard_map/ppermute | solution.py:237
  4.4 1.3 %collective-permute-start.1 = (bf16[2,128,1024]{2,1,0:T(8,128)(2,1)S(1)}, bf16[2,128,1024]{2,1,0:T(8,128)(2,1)S(1)}, u32[]{:S(2)}, u32[]{:S(2)}) collective-permute-start(bf16[2,128,1024]{2,1,0:T(8,128)(2,1)S(1)} %broadcast_select_fusion.refs_1_.refs_3_), channel_id=1, source_target_pairs={{0,1},{2,3},{4,5},{6,7},{8,9},{10,11},{12,13},{14,15},{16,17},{18,... | collective-permute-start | bytes 1572872 | tf_op jit(solution)/shard_map/ppermute | solution.py:237
  5.7 3.1 %collective-permute-start = (bf16[2,128,1024]{2,1,0:T(8,128)(2,1)S(1)}, bf16[2,128,1024]{2,1,0:T(8,128)(2,1)S(1)}, u32[]{:S(2)}, u32[]{:S(2)}) collective-permute-start(bf16[2,128,1024]{2,1,0:T(8,128)(2,1)S(1)} %broadcast_select_fusion.refs_1_.refs_3_), channel_id=1, source_target_pairs={{0,2},{1,3},{4,6},{5,7},{8,10},{9,11},{12,14},{13,15},{16,18},{17,... | collective-permute-start | bytes 1572872 | tf_op jit(solution)/shard_map/ppermute | solution.py:237
  8.8 7.0 %collective-permute-done.2.refs_3_.refs_5_ = bf16[2,128,1024]{2,1,0:T(8,128)(2,1)S(1)} collective-permute-done((bf16[2,128,1024]{2,1,0:T(8,128)(2,1)S(1)}, bf16[2,128,1024]{2,1,0:T(8,128)(2,1)S(1)}, u32[]{:S(2)}, u32[]{:S(2)}) %collective-permute-start.2) | collective-permute-done | bytes 524320 | tf_op jit(solution)/shard_map/ppermute | solution.py:237
  15.8 3.2 %collective-permute-start.4 = (bf16[2,128,1024]{2,1,0:T(8,128)(2,1)S(1)}, bf16[2,128,1024]{2,1,0:T(8,128)(2,1)S(1)}, u32[]{:S(2)}, u32[]{:S(2)}) collective-permute-start(bf16[2,128,1024]{2,1,0:T(8,128)(2,1)S(1)} %collective-permute-done.2.refs_3_.refs_5_), channel_id=1, source_target_pairs={{4,8},{5,9},{6,10},{7,11},{8,12},{9,13},{10,14},{11,15},{20,24},{2... | collective-permute-start | bytes 1572872 | tf_op jit(solution)/shard_map/ppermute | solution.py:237
  19.0 3.1 %collective-permute-start.3 = (bf16[2,128,1024]{2,1,0:T(8,128)(2,1)S(1)}, bf16[2,128,1024]{2,1,0:T(8,128)(2,1)S(1)}, u32[]{:S(2)}, u32[]{:S(2)}) collective-permute-start(bf16[2,128,1024]{2,1,0:T(8,128)(2,1)S(1)} %collective-permute-done.2.refs_3_.refs_5_), channel_id=1, source_target_pairs={{6,4},{7,5},{4,6},{5,7},{10,8},{11,9},{8,10},{9,11},{14,12},{15,13... | collective-permute-start | bytes 1572872 | tf_op jit(solution)/shard_map/ppermute | solution.py:237
  22.4 0.7 concatenate.3.info
  23.1 0.0 collective-permute-done.1.refs_2_.refs_4_
  23.1 0.0 collective-permute-done.refs_4_.refs_6_
  23.1 4.0 %collective-permute-start.6 = (bf16[2,128,1024]{2,1,0:T(8,128)(2,1)S(1)}, bf16[2,128,1024]{2,1,0:T(8,128)(2,1)S(1)}, u32[]{:S(2)}, u32[]{:S(2)}) collective-permute-start(bf16[2,128,1024]{2,1,0:T(8,128)(2,1)S(1)} %collective-permute-done.2.refs_3_.refs_5_), channel_id=1, source_target_pairs={{5,4},{4,5},{7,6},{6,7},{9,8},{8,9},{11,10},{10,11},{13,12},{12,13... | collective-permute-start | bytes 1572872 | tf_op jit(solution)/shard_map/ppermute | solution.py:237
  27.1 0.0 copy-start
  27.2 1.6 %copy-done = bf16[1,128,8192]{2,1,0:T(8,128)(2,1)S(1)} copy-done((bf16[1,128,8192]{2,1,0:T(8,128)(2,1)S(1)}, bf16[1,128,8192]{2,1,0:T(8,128)(2,1)}, u32[]{:S(2)}) %copy-start) | copy-done | bytes 2097176
  28.7 5.4 %shard_map.46 = (f32[128,8192]{1,0:T(8,128)S(1)}, f32[8,128,128]{2,1,0:T(8,128)S(1)}) custom-call(s32[22]{0:T(128)S(1)} %concatenate.3.info, bf16[128,8192]{1,0:T(8,128)(2,1)S(1)} %bitcast.19, bf16[2,128,1024]{2,1,0:T(8,128)(2,1)S(1)} %broadcast_select_fusion.refs_1_.refs_3_, bf16[2,128,1024]{2,1,0:T(8,128)(2,1)S(1)} %collective-permute-done.1.refs_2_.refs_4_, ...), custom_call_target="tpu_custom_call" | custom-call | flops 16777216 | bytes 1048576 | tf_op jit(solution)/shard_map/pallas_call | solution.py:188
  34.2 0.0 collective-permute-done.4.refs_4_.refs_8_
  34.2 0.1 broadcast_select_fusion.1
  34.2 1.9 %collective-permute-start.5 = (bf16[2,128,1024]{2,1,0:T(8,128)(2,1)S(1)}, bf16[2,128,1024]{2,1,0:T(8,128)(2,1)S(1)}, u32[]{:S(2)}, u32[]{:S(2)}) collective-permute-start(bf16[2,128,1024]{2,1,0:T(8,128)(2,1)S(1)} %broadcast_select_fusion.1), channel_id=1, source_target_pairs={{10,8},{14,12},{5,9},{9,13},{26,24},{30,28},{21,25},{25,29}} | collective-permute-start | bytes 1572872 | tf_op jit(solution)/shard_map/ppermute | solution.py:237
  36.2 2.4 %collective-permute-start.7 = (bf16[2,128,1024]{2,1,0:T(8,128)(2,1)S(1)}, bf16[2,128,1024]{2,1,0:T(8,128)(2,1)S(1)}, u32[]{:S(2)}, u32[]{:S(2)}) collective-permute-start(bf16[2,128,1024]{2,1,0:T(8,128)(2,1)S(1)} %collective-permute-done.4.refs_4_.refs_8_), channel_id=1, source_target_pairs={{9,8},{11,10},{13,12},{15,14},{25,24},{27,26},{29,28},{31,30}} | collective-permute-start | bytes 1572872 | tf_op jit(solution)/shard_map/ppermute | solution.py:237
  38.6 1.9 %collective-permute-start.9 = (bf16[2,128,1024]{2,1,0:T(8,128)(2,1)S(1)}, bf16[2,128,1024]{2,1,0:T(8,128)(2,1)S(1)}, u32[]{:S(2)}, u32[]{:S(2)}) collective-permute-start(bf16[2,128,1024]{2,1,0:T(8,128)(2,1)S(1)} %collective-permute-done.3.refs_5_.refs_9_), channel_id=1, source_target_pairs={{5,4},{4,5},{7,6},{6,7},{9,8},{8,9},{11,10},{10,11},{13,12},{12,13... | collective-permute-start | bytes 1572872 | tf_op jit(solution)/shard_map/ppermute | solution.py:237
  40.5 0.7 collective-permute-start.8
  41.2 5.5 %shard_map.47 = (f32[128,8192]{1,0:T(8,128)S(1)}, f32[8,128,128]{2,1,0:T(8,128)S(1)}) custom-call(s32[22]{0:T(128)S(1)} %concatenate.3.info, bf16[128,8192]{1,0:T(8,128)(2,1)S(1)} %bitcast.20, f32[128,8192]{1,0:T(8,128)S(1)} %get-tuple-element.25.refs_1_, f32[8,128,128]{2,1,0:T(8,128)S(1)} %get-tuple-element.26.refs_2_, ...), custom_call_target="tpu_custom_call" | custom-call | flops 16777216 | bytes 1048576 | tf_op jit(solution)/shard_map/pallas_call | solution.py:188
  46.7 2.4 %collective-permute-start.10 = (bf16[2,128,1024]{2,1,0:T(8,128)(2,1)S(1)}, bf16[2,128,1024]{2,1,0:T(8,128)(2,1)S(1)}, u32[]{:S(2)}, u32[]{:S(2)}) collective-permute-start(bf16[2,128,1024]{2,1,0:T(8,128)(2,1)S(1)} %collective-permute-done.5.refs_13_), channel_id=1, source_target_pairs={{9,8},{8,9},{13,12},{12,13},{25,24},{24,25},{29,28},{28,29}} | collective-permute-start | bytes 1572872 | tf_op jit(solution)/shard_map/ppermute | solution.py:237
  49.2 1.5 %collective-permute-done.10.refs_14_ = bf16[2,128,1024]{2,1,0:T(8,128)(2,1)S(1)} collective-permute-done((bf16[2,128,1024]{2,1,0:T(8,128)(2,1)S(1)}, bf16[2,128,1024]{2,1,0:T(8,128)(2,1)S(1)}, u32[]{:S(2)}, u32[]{:S(2)}) %collective-permute-start.10) | collective-permute-done | bytes 524320 | tf_op jit(solution)/shard_map/ppermute | solution.py:237
  50.6 52.0 %shard_map.48 = bf16[128,8192]{1,0:T(8,128)(2,1)} custom-call(s32[22]{0:T(128)S(1)} %concatenate.3.info, bf16[128,8192]{1,0:T(8,128)(2,1)S(1)} %bitcast.21, f32[128,8192]{1,0:T(8,128)S(1)} %get-tuple-element.29.refs_1_, f32[8,128,128]{2,1,0:T(8,128)S(1)} %get-tuple-element.30.refs_2_, bf16[2,128,1024]{2,1,0:T(8,128)(2,1)S(1)} %broadcast_select_fusion.refs_1_.refs_3_, ...), custom_call_target="tpu_custom_call" | custom-call | flops 16777216 | bytes 1048576 | tf_op jit(solution)/shard_map/pallas_call | solution.py:188
  (7 shorter events, 0.0 us)
Async XLA Ops:
  1.2 14.7 %collective-permute-start.2 = (bf16[2,128,1024]{2,1,0:T(8,128)(2,1)S(1)}, bf16[2,128,1024]{2,1,0:T(8,128)(2,1)S(1)}, u32[]{:S(2)}, u32[]{:S(2)}) collective-permute-start(bf16[2,128,1024]{2,1,0:T(8,128)(2,1)S(1)} %broadcast_select_fusion.refs_1_.refs_3_), channel_id=1, source_target_pairs={{0,4},{1,5},{2,6},{3,7},{4,8},{5,9},{6,10},{7,11},{8,12},{9,13},{1... | collective-permute-start | bytes 1572872 | tf_op jit(solution)/shard_map/ppermute | solution.py:237
  4.4 18.7 %collective-permute-start.1 = (bf16[2,128,1024]{2,1,0:T(8,128)(2,1)S(1)}, bf16[2,128,1024]{2,1,0:T(8,128)(2,1)S(1)}, u32[]{:S(2)}, u32[]{:S(2)}) collective-permute-start(bf16[2,128,1024]{2,1,0:T(8,128)(2,1)S(1)} %broadcast_select_fusion.refs_1_.refs_3_), channel_id=1, source_target_pairs={{0,1},{2,3},{4,5},{6,7},{8,9},{10,11},{12,13},{14,15},{16,17},{18,... | collective-permute-start | bytes 1572872 | tf_op jit(solution)/shard_map/ppermute | solution.py:237
  5.7 17.4 %collective-permute-start = (bf16[2,128,1024]{2,1,0:T(8,128)(2,1)S(1)}, bf16[2,128,1024]{2,1,0:T(8,128)(2,1)S(1)}, u32[]{:S(2)}, u32[]{:S(2)}) collective-permute-start(bf16[2,128,1024]{2,1,0:T(8,128)(2,1)S(1)} %broadcast_select_fusion.refs_1_.refs_3_), channel_id=1, source_target_pairs={{0,2},{1,3},{4,6},{5,7},{8,10},{9,11},{12,14},{13,15},{16,18},{17,... | collective-permute-start | bytes 1572872 | tf_op jit(solution)/shard_map/ppermute | solution.py:237
  15.8 18.3 %collective-permute-start.4 = (bf16[2,128,1024]{2,1,0:T(8,128)(2,1)S(1)}, bf16[2,128,1024]{2,1,0:T(8,128)(2,1)S(1)}, u32[]{:S(2)}, u32[]{:S(2)}) collective-permute-start(bf16[2,128,1024]{2,1,0:T(8,128)(2,1)S(1)} %collective-permute-done.2.refs_3_.refs_5_), channel_id=1, source_target_pairs={{4,8},{5,9},{6,10},{7,11},{8,12},{9,13},{10,14},{11,15},{20,24},{2... | collective-permute-start | bytes 1572872 | tf_op jit(solution)/shard_map/ppermute | solution.py:237
  19.0 15.1 %collective-permute-start.3 = (bf16[2,128,1024]{2,1,0:T(8,128)(2,1)S(1)}, bf16[2,128,1024]{2,1,0:T(8,128)(2,1)S(1)}, u32[]{:S(2)}, u32[]{:S(2)}) collective-permute-start(bf16[2,128,1024]{2,1,0:T(8,128)(2,1)S(1)} %collective-permute-done.2.refs_3_.refs_5_), channel_id=1, source_target_pairs={{6,4},{7,5},{4,6},{5,7},{10,8},{11,9},{8,10},{9,11},{14,12},{15,13... | collective-permute-start | bytes 1572872 | tf_op jit(solution)/shard_map/ppermute | solution.py:237
  23.1 18.1 %collective-permute-start.6 = (bf16[2,128,1024]{2,1,0:T(8,128)(2,1)S(1)}, bf16[2,128,1024]{2,1,0:T(8,128)(2,1)S(1)}, u32[]{:S(2)}, u32[]{:S(2)}) collective-permute-start(bf16[2,128,1024]{2,1,0:T(8,128)(2,1)S(1)} %collective-permute-done.2.refs_3_.refs_5_), channel_id=1, source_target_pairs={{5,4},{4,5},{7,6},{6,7},{9,8},{8,9},{11,10},{10,11},{13,12},{12,13... | collective-permute-start | bytes 1572872 | tf_op jit(solution)/shard_map/ppermute | solution.py:237
  27.1 1.6 %copy-start = (bf16[1,128,8192]{2,1,0:T(8,128)(2,1)S(1)}, bf16[1,128,8192]{2,1,0:T(8,128)(2,1)}, u32[]{:S(2)}) copy-start(bf16[1,128,8192]{2,1,0:T(8,128)(2,1)} %param.4) | copy-start | bytes 6291460
  34.2 12.5 %collective-permute-start.5 = (bf16[2,128,1024]{2,1,0:T(8,128)(2,1)S(1)}, bf16[2,128,1024]{2,1,0:T(8,128)(2,1)S(1)}, u32[]{:S(2)}, u32[]{:S(2)}) collective-permute-start(bf16[2,128,1024]{2,1,0:T(8,128)(2,1)S(1)} %broadcast_select_fusion.1), channel_id=1, source_target_pairs={{10,8},{14,12},{5,9},{9,13},{26,24},{30,28},{21,25},{25,29}} | collective-permute-start | bytes 1572872 | tf_op jit(solution)/shard_map/ppermute | solution.py:237
  36.2 13.0 %collective-permute-start.7 = (bf16[2,128,1024]{2,1,0:T(8,128)(2,1)S(1)}, bf16[2,128,1024]{2,1,0:T(8,128)(2,1)S(1)}, u32[]{:S(2)}, u32[]{:S(2)}) collective-permute-start(bf16[2,128,1024]{2,1,0:T(8,128)(2,1)S(1)} %collective-permute-done.4.refs_4_.refs_8_), channel_id=1, source_target_pairs={{9,8},{11,10},{13,12},{15,14},{25,24},{27,26},{29,28},{31,30}} | collective-permute-start | bytes 1572872 | tf_op jit(solution)/shard_map/ppermute | solution.py:237
  38.6 10.6 %collective-permute-start.9 = (bf16[2,128,1024]{2,1,0:T(8,128)(2,1)S(1)}, bf16[2,128,1024]{2,1,0:T(8,128)(2,1)S(1)}, u32[]{:S(2)}, u32[]{:S(2)}) collective-permute-start(bf16[2,128,1024]{2,1,0:T(8,128)(2,1)S(1)} %collective-permute-done.3.refs_5_.refs_9_), channel_id=1, source_target_pairs={{5,4},{4,5},{7,6},{6,7},{9,8},{8,9},{11,10},{10,11},{13,12},{12,13... | collective-permute-start | bytes 1572872 | tf_op jit(solution)/shard_map/ppermute | solution.py:237
  40.5 8.6 %collective-permute-start.8 = (bf16[2,128,1024]{2,1,0:T(8,128)(2,1)S(1)}, bf16[2,128,1024]{2,1,0:T(8,128)(2,1)S(1)}, u32[]{:S(2)}, u32[]{:S(2)}) collective-permute-start(bf16[2,128,1024]{2,1,0:T(8,128)(2,1)S(1)} %collective-permute-done.refs_4_.refs_6_), channel_id=1, source_target_pairs={{3,2},{2,3},{7,6},{6,7},{11,10},{10,11},{15,14},{14,15},{19,18},{1... | collective-permute-start | bytes 1572872 | tf_op jit(solution)/shard_map/ppermute | solution.py:237
  46.7 3.9 %collective-permute-start.10 = (bf16[2,128,1024]{2,1,0:T(8,128)(2,1)S(1)}, bf16[2,128,1024]{2,1,0:T(8,128)(2,1)S(1)}, u32[]{:S(2)}, u32[]{:S(2)}) collective-permute-start(bf16[2,128,1024]{2,1,0:T(8,128)(2,1)S(1)} %collective-permute-done.5.refs_13_), channel_id=1, source_target_pairs={{9,8},{8,9},{13,12},{12,13},{25,24},{24,25},{29,28},{28,29}} | collective-permute-start | bytes 1572872 | tf_op jit(solution)/shard_map/ppermute | solution.py:237

commit v5 on v4

--- a/solution.py
+++ b/solution.py
@@ -90,19 +90,22 @@
                     ahead.append(score(pieces[i + 1], tile))
             v = [jnp.concatenate([kv_refs[array][1, :, span(g, d)], one], axis=1) for _, array in part]
             o = jnp.dot(jnp.concatenate(p, axis=1), jnp.concatenate(v, axis=0), preferred_element_type=jnp.float32)
-            for n in range(rows // tok):
-                j = first // tok + n
-                acc, row_sum = o[n * tok:(n + 1) * tok, :d], o[n * tok:(n + 1) * tok, d:]
-                if has_state:
-                    acc = acc + state[0][:, span(g * GROUP + j, d)]
+            heads = range(first // tok, (first + rows) // tok)
+            accs = [o[n * tok:(n + 1) * tok, :d] for n in range(len(heads))]
+            if has_state:
+                accs = [acc + state[0][:, span(g * GROUP + j, d)] for acc, j in zip(accs, heads)]
+            for n, j in enumerate(heads):
+                packed[h] = jnp.where(lane == j, o[n * tok:(n + 1) * tok, d:], packed[h])
+            if is_last:
+                row_sum = packed[h] + state[1][g]
+                row_sum = jnp.where((lane >= heads[0]) & (lane <= heads[-1]), row_sum, 1.0)
+                least, most = jnp.minimum(least, row_sum), jnp.maximum(most, row_sum)
+                share = pl.reciprocal(row_sum, approx=True)
+                share = share * (2.0 - row_sum * share)
+            for acc, j in zip(accs, heads):
                 if is_last:
-                    row_sum = row_sum + state[1][g, :, j:j + 1]
-                    least, most = jnp.minimum(least, row_sum), jnp.maximum(most, row_sum)
-                    share = pl.reciprocal(row_sum, approx=True)
-                    share = share * (2.0 - row_sum * share)
-                    out_buf[buf, h, :, j * d:(j + 1) * d] = (acc * share).astype(jnp.bfloat16)
+                    out_buf[buf, h, :, j * d:(j + 1) * d] = (acc * share[:, j:j + 1]).astype(jnp.bfloat16)
                 else:
-                    packed[h] = jnp.where(lane == j, row_sum, packed[h])
                     acc_ref[:, span(g * GROUP + j, d)] = acc
             if is_last and first + rows == GROUP * tok:
                 result(u, buf, h).start()
@@ -263,11 +266,11 @@
         for dx in columns:
             pairs = self.across(reach, dx, (0,)) + self.climb(dx, (1,))
             got[reach, dx, 0] = send(jnp.where(core == 0, got[reach, 0, 0], got[reach - 1, dx, 0]), pairs)
+        for dx in columns:
+            for level in reversed(range(reach)):
+                swap(level, dx)
         for level in range(2, reach + 1):
             swap(level, 0)
-        for dx in columns:
-            for level in range(reach):
-                swap(level, dx)
         state, = tie([(reach, dx, 0) for dx in columns], attend_middle(got, state))
         for dx in columns:
             swap(reach, dx)

time: 103 us -> 103 us (level)
  no operation moved by 1% of the time
where the time goes in v5:
time: 103 us
  Pallas kernels  63 us (61%)
  starting transfers between devices  27.3 us (27%)
  waiting for transfers between devices  8.52 us (8%)
  local copies, waits for them, and re-layouts  2.33 us (2%)
  other arithmetic  1.21 us (1%)
    pallas_call x3, Pallas kernels, attend(): pl.pallas_call(functools.partial(kernel, form), out_shape=outs, in_specs=...  63 us
    ppermute x11, starting transfers between devices, carry(): send = lambda array, pairs: lax.ppermute(array, 'head', pairs)  27.3 us
    ppermute x11, waiting for transfers between devices, carry(): send = lambda array, pairs: lax.ppermute(array, 'head', pairs)  8.52 us
  transfers between devices with their start and end apart: 11, of which 2 were waited for; matrix products, arithmetic and copies ran while one was open for 1% of the time, Pallas kernels for 11%

profile of v5, /device:TPU:17, one launch (start us, length us, event | category | flops | bytes accessed | tf_op | source)
XLA Modules:
  0.0 102.9 jit_solution(8437995031749012886)
XLA Ops:
  0.0 1.1 %broadcast_select_fusion.refs_1_.refs_3_ = bf16[2,128,1024]{2,1,0:T(8,128)(2,1)S(1)} fusion(pred[2]{0:T(512)(128)(4,1)S(1)} %iota_compare_fusion, bf16[128,1024]{1,0:T(8,128)(2,1)} %bitcast.22, bf16[128,1024]{1,0:T(8,128)(2,1)} %bitcast.23), kind=kLoop, calls=%fused_computation | loop fusion | flops 262144 | bytes 1048578 | tf_op jit(solution)/shard_map/jit(_where)/select_n | solution.py:205
  1.2 3.2 %collective-permute-start.2 = (bf16[2,128,1024]{2,1,0:T(8,128)(2,1)S(1)}, bf16[2,128,1024]{2,1,0:T(8,128)(2,1)S(1)}, u32[]{:S(2)}, u32[]{:S(2)}) collective-permute-start(bf16[2,128,1024]{2,1,0:T(8,128)(2,1)S(1)} %broadcast_select_fusion.refs_1_.refs_3_), channel_id=1, source_target_pairs={{0,4},{1,5},{2,6},{3,7},{4,8},{5,9},{6,10},{7,11},{8,12},{9,13},{1... | collective-permute-start | bytes 1572872 | tf_op jit(solution)/shard_map/ppermute | solution.py:240
  4.4 1.3 %collective-permute-start.1 = (bf16[2,128,1024]{2,1,0:T(8,128)(2,1)S(1)}, bf16[2,128,1024]{2,1,0:T(8,128)(2,1)S(1)}, u32[]{:S(2)}, u32[]{:S(2)}) collective-permute-start(bf16[2,128,1024]{2,1,0:T(8,128)(2,1)S(1)} %broadcast_select_fusion.refs_1_.refs_3_), channel_id=1, source_target_pairs={{0,1},{2,3},{4,5},{6,7},{8,9},{10,11},{12,13},{14,15},{16,17},{18,... | collective-permute-start | bytes 1572872 | tf_op jit(solution)/shard_map/ppermute | solution.py:240
  5.7 3.1 %collective-permute-start = (bf16[2,128,1024]{2,1,0:T(8,128)(2,1)S(1)}, bf16[2,128,1024]{2,1,0:T(8,128)(2,1)S(1)}, u32[]{:S(2)}, u32[]{:S(2)}) collective-permute-start(bf16[2,128,1024]{2,1,0:T(8,128)(2,1)S(1)} %broadcast_select_fusion.refs_1_.refs_3_), channel_id=1, source_target_pairs={{0,2},{1,3},{4,6},{5,7},{8,10},{9,11},{12,14},{13,15},{16,18},{17,... | collective-permute-start | bytes 1572872 | tf_op jit(solution)/shard_map/ppermute | solution.py:240
  8.8 7.0 %collective-permute-done.2.refs_3_.refs_5_ = bf16[2,128,1024]{2,1,0:T(8,128)(2,1)S(1)} collective-permute-done((bf16[2,128,1024]{2,1,0:T(8,128)(2,1)S(1)}, bf16[2,128,1024]{2,1,0:T(8,128)(2,1)S(1)}, u32[]{:S(2)}, u32[]{:S(2)}) %collective-permute-start.2) | collective-permute-done | bytes 524320 | tf_op jit(solution)/shard_map/ppermute | solution.py:240
  15.8 3.2 %collective-permute-start.4 = (bf16[2,128,1024]{2,1,0:T(8,128)(2,1)S(1)}, bf16[2,128,1024]{2,1,0:T(8,128)(2,1)S(1)}, u32[]{:S(2)}, u32[]{:S(2)}) collective-permute-start(bf16[2,128,1024]{2,1,0:T(8,128)(2,1)S(1)} %collective-permute-done.2.refs_3_.refs_5_), channel_id=1, source_target_pairs={{4,8},{5,9},{6,10},{7,11},{8,12},{9,13},{10,14},{11,15},{20,24},{2... | collective-permute-start | bytes 1572872 | tf_op jit(solution)/shard_map/ppermute | solution.py:240
  19.0 3.1 %collective-permute-start.3 = (bf16[2,128,1024]{2,1,0:T(8,128)(2,1)S(1)}, bf16[2,128,1024]{2,1,0:T(8,128)(2,1)S(1)}, u32[]{:S(2)}, u32[]{:S(2)}) collective-permute-start(bf16[2,128,1024]{2,1,0:T(8,128)(2,1)S(1)} %collective-permute-done.2.refs_3_.refs_5_), channel_id=1, source_target_pairs={{6,4},{7,5},{4,6},{5,7},{10,8},{11,9},{8,10},{9,11},{14,12},{15,13... | collective-permute-start | bytes 1572872 | tf_op jit(solution)/shard_map/ppermute | solution.py:240
  22.4 0.7 concatenate.3.info
  23.1 0.0 collective-permute-done.1.refs_2_.refs_4_
  23.1 4.0 %collective-permute-start.6 = (bf16[2,128,1024]{2,1,0:T(8,128)(2,1)S(1)}, bf16[2,128,1024]{2,1,0:T(8,128)(2,1)S(1)}, u32[]{:S(2)}, u32[]{:S(2)}) collective-permute-start(bf16[2,128,1024]{2,1,0:T(8,128)(2,1)S(1)} %collective-permute-done.2.refs_3_.refs_5_), channel_id=1, source_target_pairs={{5,4},{4,5},{7,6},{6,7},{9,8},{8,9},{11,10},{10,11},{13,12},{12,13... | collective-permute-start | bytes 1572872 | tf_op jit(solution)/shard_map/ppermute | solution.py:240
  27.1 0.0 copy-start
  27.2 1.6 %copy-done = bf16[1,128,8192]{2,1,0:T(8,128)(2,1)S(1)} copy-done((bf16[1,128,8192]{2,1,0:T(8,128)(2,1)S(1)}, bf16[1,128,8192]{2,1,0:T(8,128)(2,1)}, u32[]{:S(2)}) %copy-start) | copy-done | bytes 2097176
  28.7 5.4 %shard_map.46 = (f32[128,8192]{1,0:T(8,128)S(1)}, f32[8,128,128]{2,1,0:T(8,128)S(1)}) custom-call(s32[22]{0:T(128)S(1)} %concatenate.3.info, bf16[128,8192]{1,0:T(8,128)(2,1)S(1)} %bitcast.19, bf16[2,128,1024]{2,1,0:T(8,128)(2,1)S(1)} %broadcast_select_fusion.refs_1_.refs_3_, bf16[2,128,1024]{2,1,0:T(8,128)(2,1)S(1)} %collective-permute-done.1.refs_2_.refs_4_, ...), custom_call_target="tpu_custom_call" | custom-call | flops 16777216 | bytes 1048576 | tf_op jit(solution)/shard_map/pallas_call | solution.py:191
  34.2 0.0 collective-permute-done.4.refs_4_.refs_8_
  34.2 0.0 collective-permute-done.3.refs_5_.refs_9_
  34.2 0.1 broadcast_select_fusion.1
  34.2 1.9 %collective-permute-start.5 = (bf16[2,128,1024]{2,1,0:T(8,128)(2,1)S(1)}, bf16[2,128,1024]{2,1,0:T(8,128)(2,1)S(1)}, u32[]{:S(2)}, u32[]{:S(2)}) collective-permute-start(bf16[2,128,1024]{2,1,0:T(8,128)(2,1)S(1)} %broadcast_select_fusion.1), channel_id=1, source_target_pairs={{10,8},{14,12},{5,9},{9,13},{26,24},{30,28},{21,25},{25,29}} | collective-permute-start | bytes 1572872 | tf_op jit(solution)/shard_map/ppermute | solution.py:240
  36.2 2.4 %collective-permute-start.7 = (bf16[2,128,1024]{2,1,0:T(8,128)(2,1)S(1)}, bf16[2,128,1024]{2,1,0:T(8,128)(2,1)S(1)}, u32[]{:S(2)}, u32[]{:S(2)}) collective-permute-start(bf16[2,128,1024]{2,1,0:T(8,128)(2,1)S(1)} %collective-permute-done.4.refs_4_.refs_8_), channel_id=1, source_target_pairs={{9,8},{11,10},{13,12},{15,14},{25,24},{27,26},{29,28},{31,30}} | collective-permute-start | bytes 1572872 | tf_op jit(solution)/shard_map/ppermute | solution.py:240
  38.6 1.9 %collective-permute-start.9 = (bf16[2,128,1024]{2,1,0:T(8,128)(2,1)S(1)}, bf16[2,128,1024]{2,1,0:T(8,128)(2,1)S(1)}, u32[]{:S(2)}, u32[]{:S(2)}) collective-permute-start(bf16[2,128,1024]{2,1,0:T(8,128)(2,1)S(1)} %collective-permute-done.3.refs_5_.refs_9_), channel_id=1, source_target_pairs={{5,4},{4,5},{7,6},{6,7},{9,8},{8,9},{11,10},{10,11},{13,12},{12,13... | collective-permute-start | bytes 1572872 | tf_op jit(solution)/shard_map/ppermute | solution.py:240
  40.5 0.7 collective-permute-start.8
  41.2 5.5 %shard_map.47 = (f32[128,8192]{1,0:T(8,128)S(1)}, f32[8,128,128]{2,1,0:T(8,128)S(1)}) custom-call(s32[22]{0:T(128)S(1)} %concatenate.3.info, bf16[128,8192]{1,0:T(8,128)(2,1)S(1)} %bitcast.20, f32[128,8192]{1,0:T(8,128)S(1)} %get-tuple-element.25.refs_1_, f32[8,128,128]{2,1,0:T(8,128)S(1)} %get-tuple-element.26.refs_2_, ...), custom_call_target="tpu_custom_call" | custom-call | flops 16777216 | bytes 1048576 | tf_op jit(solution)/shard_map/pallas_call | solution.py:191
  46.7 2.4 %collective-permute-start.10 = (bf16[2,128,1024]{2,1,0:T(8,128)(2,1)S(1)}, bf16[2,128,1024]{2,1,0:T(8,128)(2,1)S(1)}, u32[]{:S(2)}, u32[]{:S(2)}) collective-permute-start(bf16[2,128,1024]{2,1,0:T(8,128)(2,1)S(1)} %collective-permute-done.5.refs_13_), channel_id=1, source_target_pairs={{9,8},{8,9},{13,12},{12,13},{25,24},{24,25},{29,28},{28,29}} | collective-permute-start | bytes 1572872 | tf_op jit(solution)/shard_map/ppermute | solution.py:240
  49.2 1.5 %collective-permute-done.10.refs_14_ = bf16[2,128,1024]{2,1,0:T(8,128)(2,1)S(1)} collective-permute-done((bf16[2,128,1024]{2,1,0:T(8,128)(2,1)S(1)}, bf16[2,128,1024]{2,1,0:T(8,128)(2,1)S(1)}, u32[]{:S(2)}, u32[]{:S(2)}) %collective-permute-start.10) | collective-permute-done | bytes 524320 | tf_op jit(solution)/shard_map/ppermute | solution.py:240
  50.6 52.1 %shard_map.48 = bf16[128,8192]{1,0:T(8,128)(2,1)} custom-call(s32[22]{0:T(128)S(1)} %concatenate.3.info, bf16[128,8192]{1,0:T(8,128)(2,1)S(1)} %bitcast.21, f32[128,8192]{1,0:T(8,128)S(1)} %get-tuple-element.29.refs_1_, f32[8,128,128]{2,1,0:T(8,128)S(1)} %get-tuple-element.30.refs_2_, bf16[2,128,1024]{2,1,0:T(8,128)(2,1)S(1)} %broadcast_select_fusion.refs_1_.refs_3_, ...), custom_call_target="tpu_custom_call" | custom-call | flops 16777216 | bytes 1048576 | tf_op jit(solution)/shard_map/pallas_call | solution.py:191
  (7 shorter events, 0.0 us)
Async XLA Ops:
  1.2 14.7 %collective-permute-start.2 = (bf16[2,128,1024]{2,1,0:T(8,128)(2,1)S(1)}, bf16[2,128,1024]{2,1,0:T(8,128)(2,1)S(1)}, u32[]{:S(2)}, u32[]{:S(2)}) collective-permute-start(bf16[2,128,1024]{2,1,0:T(8,128)(2,1)S(1)} %broadcast_select_fusion.refs_1_.refs_3_), channel_id=1, source_target_pairs={{0,4},{1,5},{2,6},{3,7},{4,8},{5,9},{6,10},{7,11},{8,12},{9,13},{1... | collective-permute-start | bytes 1572872 | tf_op jit(solution)/shard_map/ppermute | solution.py:240
  4.4 18.7 %collective-permute-start.1 = (bf16[2,128,1024]{2,1,0:T(8,128)(2,1)S(1)}, bf16[2,128,1024]{2,1,0:T(8,128)(2,1)S(1)}, u32[]{:S(2)}, u32[]{:S(2)}) collective-permute-start(bf16[2,128,1024]{2,1,0:T(8,128)(2,1)S(1)} %broadcast_select_fusion.refs_1_.refs_3_), channel_id=1, source_target_pairs={{0,1},{2,3},{4,5},{6,7},{8,9},{10,11},{12,13},{14,15},{16,17},{18,... | collective-permute-start | bytes 1572872 | tf_op jit(solution)/shard_map/ppermute | solution.py:240
  5.7 17.4 %collective-permute-start = (bf16[2,128,1024]{2,1,0:T(8,128)(2,1)S(1)}, bf16[2,128,1024]{2,1,0:T(8,128)(2,1)S(1)}, u32[]{:S(2)}, u32[]{:S(2)}) collective-permute-start(bf16[2,128,1024]{2,1,0:T(8,128)(2,1)S(1)} %broadcast_select_fusion.refs_1_.refs_3_), channel_id=1, source_target_pairs={{0,2},{1,3},{4,6},{5,7},{8,10},{9,11},{12,14},{13,15},{16,18},{17,... | collective-permute-start | bytes 1572872 | tf_op jit(solution)/shard_map/ppermute | solution.py:240
  15.8 18.3 %collective-permute-start.4 = (bf16[2,128,1024]{2,1,0:T(8,128)(2,1)S(1)}, bf16[2,128,1024]{2,1,0:T(8,128)(2,1)S(1)}, u32[]{:S(2)}, u32[]{:S(2)}) collective-permute-start(bf16[2,128,1024]{2,1,0:T(8,128)(2,1)S(1)} %collective-permute-done.2.refs_3_.refs_5_), channel_id=1, source_target_pairs={{4,8},{5,9},{6,10},{7,11},{8,12},{9,13},{10,14},{11,15},{20,24},{2... | collective-permute-start | bytes 1572872 | tf_op jit(solution)/shard_map/ppermute | solution.py:240
  19.0 15.1 %collective-permute-start.3 = (bf16[2,128,1024]{2,1,0:T(8,128)(2,1)S(1)}, bf16[2,128,1024]{2,1,0:T(8,128)(2,1)S(1)}, u32[]{:S(2)}, u32[]{:S(2)}) collective-permute-start(bf16[2,128,1024]{2,1,0:T(8,128)(2,1)S(1)} %collective-permute-done.2.refs_3_.refs_5_), channel_id=1, source_target_pairs={{6,4},{7,5},{4,6},{5,7},{10,8},{11,9},{8,10},{9,11},{14,12},{15,13... | collective-permute-start | bytes 1572872 | tf_op jit(solution)/shard_map/ppermute | solution.py:240
  23.1 18.1 %collective-permute-start.6 = (bf16[2,128,1024]{2,1,0:T(8,128)(2,1)S(1)}, bf16[2,128,1024]{2,1,0:T(8,128)(2,1)S(1)}, u32[]{:S(2)}, u32[]{:S(2)}) collective-permute-start(bf16[2,128,1024]{2,1,0:T(8,128)(2,1)S(1)} %collective-permute-done.2.refs_3_.refs_5_), channel_id=1, source_target_pairs={{5,4},{4,5},{7,6},{6,7},{9,8},{8,9},{11,10},{10,11},{13,12},{12,13... | collective-permute-start | bytes 1572872 | tf_op jit(solution)/shard_map/ppermute | solution.py:240
  27.1 1.6 %copy-start = (bf16[1,128,8192]{2,1,0:T(8,128)(2,1)S(1)}, bf16[1,128,8192]{2,1,0:T(8,128)(2,1)}, u32[]{:S(2)}) copy-start(bf16[1,128,8192]{2,1,0:T(8,128)(2,1)} %param.4) | copy-start | bytes 6291460
  34.2 12.5 %collective-permute-start.5 = (bf16[2,128,1024]{2,1,0:T(8,128)(2,1)S(1)}, bf16[2,128,1024]{2,1,0:T(8,128)(2,1)S(1)}, u32[]{:S(2)}, u32[]{:S(2)}) collective-permute-start(bf16[2,128,1024]{2,1,0:T(8,128)(2,1)S(1)} %broadcast_select_fusion.1), channel_id=1, source_target_pairs={{10,8},{14,12},{5,9},{9,13},{26,24},{30,28},{21,25},{25,29}} | collective-permute-start | bytes 1572872 | tf_op jit(solution)/shard_map/ppermute | solution.py:240
  36.2 13.0 %collective-permute-start.7 = (bf16[2,128,1024]{2,1,0:T(8,128)(2,1)S(1)}, bf16[2,128,1024]{2,1,0:T(8,128)(2,1)S(1)}, u32[]{:S(2)}, u32[]{:S(2)}) collective-permute-start(bf16[2,128,1024]{2,1,0:T(8,128)(2,1)S(1)} %collective-permute-done.4.refs_4_.refs_8_), channel_id=1, source_target_pairs={{9,8},{11,10},{13,12},{15,14},{25,24},{27,26},{29,28},{31,30}} | collective-permute-start | bytes 1572872 | tf_op jit(solution)/shard_map/ppermute | solution.py:240
  38.6 10.6 %collective-permute-start.9 = (bf16[2,128,1024]{2,1,0:T(8,128)(2,1)S(1)}, bf16[2,128,1024]{2,1,0:T(8,128)(2,1)S(1)}, u32[]{:S(2)}, u32[]{:S(2)}) collective-permute-start(bf16[2,128,1024]{2,1,0:T(8,128)(2,1)S(1)} %collective-permute-done.3.refs_5_.refs_9_), channel_id=1, source_target_pairs={{5,4},{4,5},{7,6},{6,7},{9,8},{8,9},{11,10},{10,11},{13,12},{12,13... | collective-permute-start | bytes 1572872 | tf_op jit(solution)/shard_map/ppermute | solution.py:240
  40.5 8.6 %collective-permute-start.8 = (bf16[2,128,1024]{2,1,0:T(8,128)(2,1)S(1)}, bf16[2,128,1024]{2,1,0:T(8,128)(2,1)S(1)}, u32[]{:S(2)}, u32[]{:S(2)}) collective-permute-start(bf16[2,128,1024]{2,1,0:T(8,128)(2,1)S(1)} %collective-permute-done.refs_4_.refs_6_), channel_id=1, source_target_pairs={{3,2},{2,3},{7,6},{6,7},{11,10},{10,11},{15,14},{14,15},{19,18},{1... | collective-permute-start | bytes 1572872 | tf_op jit(solution)/shard_map/ppermute | solution.py:240
  46.7 3.9 %collective-permute-start.10 = (bf16[2,128,1024]{2,1,0:T(8,128)(2,1)S(1)}, bf16[2,128,1024]{2,1,0:T(8,128)(2,1)S(1)}, u32[]{:S(2)}, u32[]{:S(2)}) collective-permute-start(bf16[2,128,1024]{2,1,0:T(8,128)(2,1)S(1)} %collective-permute-done.5.refs_13_), channel_id=1, source_target_pairs={{9,8},{8,9},{13,12},{12,13},{25,24},{24,25},{29,28},{28,29}} | collective-permute-start | bytes 1572872 | tf_op jit(solution)/shard_map/ppermute | solution.py:240

commit v6 on v4

--- a/solution.py
+++ b/solution.py
@@ -1,4 +1,5 @@
 import functools
+import itertools
 import math
 
 import jax
@@ -62,8 +63,12 @@
         return jnp.concatenate([jnp.concatenate([q_ref[:, span(g * GROUP + j, d)], eye], axis=1)
                                 for j in range(first // tok, (first + rows) // tok)], axis=0)
 
-    def result(u, buf, h):
-        return pltpu.make_async_copy(out_buf.at[buf, h], out_ref.at[:, span(u * UNIT + h, wide)], sems.at[buf, h])
+    def results(u, buf, h):
+        share = rows * d // tok
+        for n in range(wide // share):
+            yield pltpu.make_async_copy(out_buf.at[buf, h, :, n * share:(n + 1) * share],
+                                        out_ref.at[:, span((u * UNIT + h) * (wide // share) + n, share)],
+                                        sems.at[buf, h, n])
 
     def attend(part, u, buf):
         keys = len(part) * tok
@@ -104,8 +109,8 @@
                 else:
                     packed[h] = jnp.where(lane == j, row_sum, packed[h])
                     acc_ref[:, span(g * GROUP + j, d)] = acc
-            if is_last and first + rows == GROUP * tok:
-                result(u, buf, h).start()
+            if is_last:
+                next(itertools.islice(results(u, buf, h), first // rows, None)).start()
         if is_last:
             limits[0] = jnp.minimum(limits[0], least)
             limits[1] = jnp.maximum(limits[1], most)
@@ -126,15 +131,12 @@
                 @pl.when(u > 1)
                 def _():
                     for h in range(UNIT):
-                        result(u - 2, buf, h).wait()
+                        for copy in results(u - 2, buf, h):
+                            copy.wait()
             attend(part, u, buf)
             return carry
 
         lax.fori_loop(0, units, step, 0)
-        if is_last:
-            for u in range(units - 2, units):
-                for h in range(UNIT):
-                    result(u, u % 2, h).wait()
 
     if cut is None:
         run(slots)
@@ -144,8 +146,13 @@
 
     if is_last:
         inside = (limits[0] >= LOWEST) & (limits[1] <= HIGHEST)
-
-        @pl.when(jnp.max(jnp.where(inside, 0.0, 1.0)) > 0.0)
+        beyond = jnp.max(jnp.where(inside, 0.0, 1.0)) > 0.0
+        for u in range(KV_HEADS // UNIT - 2, KV_HEADS // UNIT):
+            for h in range(UNIT):
+                for copy in results(u, u % 2, h):
+                    copy.wait()
+
+        @pl.when(beyond)
         def _():
             for n, mask in enumerate(masks(before + slots, info, total, docs, tok)):
                 everything[0, n * tok:(n + 1) * tok, d:] = mask
@@ -154,7 +161,7 @@
             def again(g, carry):
                 for n, (_, array) in enumerate(before + slots):
                     copy = pltpu.make_async_copy(kv_refs[array].at[:, :, span(g, d)],
-                                                 everything.at[:, n * tok:(n + 1) * tok, :d], sems.at[0, 0])
+                                                 everything.at[:, n * tok:(n + 1) * tok, :d], sems.at[0, 0, 0])
                     copy.start()
                     copy.wait()
                 for j in range(GROUP):
@@ -163,7 +170,7 @@
                     p = jnp.exp2((s - top) * SCALE).astype(jnp.bfloat16)
                     o = jnp.dot(p, everything[1], preferred_element_type=jnp.float32)
                     out_buf[0, 0, :, j * d:(j + 1) * d] = (o[:, :d] / o[:, d:]).astype(jnp.bfloat16)
-                store = pltpu.make_async_copy(out_buf.at[0, 0], out_ref.at[:, span(g, wide)], sems.at[0, 0])
+                store = pltpu.make_async_copy(out_buf.at[0, 0], out_ref.at[:, span(g, wide)], sems.at[0, 0, 0])
                 store.start()
                 store.wait()
                 return carry
@@ -182,7 +189,7 @@
             pltpu.VMEM((2, UNIT, tok, GROUP * d), jnp.bfloat16),
             pltpu.VMEM((2, tok, d), jnp.float32),
             pltpu.VMEM((2, total * tok, 2 * d), jnp.bfloat16),
-            pltpu.SemaphoreType.DMA((2, UNIT)),
+            pltpu.SemaphoreType.DMA((2, UNIT, GROUP * tok // rows)),
         ]
     mine = {array for _, array in slots}
     return pl.pallas_call(
@@ -192,7 +199,7 @@
         + [here if i in mine else anywhere for i in range(len(arrays))],
         out_specs=[anywhere if is_last else here] * len(outs),
         scratch_shapes=scratch,
-        compiler_params=pltpu.CompilerParams(vmem_limit_bytes=(16 if total <= 16 else 60) * 1024 * 1024),
+        compiler_params=pltpu.CompilerParams(vmem_limit_bytes=(24 if total <= 16 else 60) * 1024 * 1024),
         cost_estimate=pl.CostEstimate(flops=COST * q.size, bytes_accessed=q.size, transcendentals=0),
     )(info, q, *state, *arrays)
 
@@ -231,7 +238,7 @@
 
     def over(self, level, dx, cores=(0, 1)):
         return [(self.at(z, x, 1 - c), self.at(z, x, c)) for z, x, c in self.everyone(level, cores)
-                if (self.wanted(level, 1 - c, c) if dx == 0 else self.wanted(level, (x - dx) % self.cols, x))]
+                if (level or c if dx == 0 else self.wanted(level, (x - dx) % self.cols, x))]
 
     def carry(self, block, core, attend_early, attend_middle):
         send = lambda array, pairs: lax.ppermute(array, "head", pairs)
@@ -302,7 +309,7 @@
     info = jnp.stack(base + [me * tok, me % route.plane // 2])
     info = jnp.concatenate([info, lengths[0]]).astype(jnp.int32)
     q = query[0]
-    rows = 512 if total <= 16 else 128
+    rows = 1024 if total <= 16 else 128
 
     def forms(part):
         if route.cols != 2 or all(name[1] == 0 or 0 < name[0] < route.reach for name in part):

time: 103 us -> 103 us (level)
  no operation moved by 1% of the time
where the time goes in v6:
time: 103 us
  Pallas kernels  62.9 us (61%)
  starting transfers between devices  27.3 us (27%)
  waiting for transfers between devices  8.52 us (8%)
  local copies, waits for them, and re-layouts  2.33 us (2%)
  other arithmetic  1.21 us (1%)
    pallas_call x3, Pallas kernels, attend(): pl.pallas_call(functools.partial(kernel, form), out_shape=outs, in_specs=...  62.9 us
    ppermute x11, starting transfers between devices, carry(): send = lambda array, pairs: lax.ppermute(array, 'head', pairs)  27.3 us
    ppermute x11, waiting for transfers between devices, carry(): send = lambda array, pairs: lax.ppermute(array, 'head', pairs)  8.52 us
  transfers between devices with their start and end apart: 11, of which 2 were waited for; matrix products, arithmetic and copies ran while one was open for 1% of the time, Pallas kernels for 11%

profile of v6, /device:TPU:17, one launch (start us, length us, event | category | flops | bytes accessed | tf_op | source)
XLA Modules:
  0.0 102.8 jit_solution(5910472684828353366)
XLA Ops:
  0.0 1.1 %broadcast_select_fusion.refs_1_.refs_3_ = bf16[2,128,1024]{2,1,0:T(8,128)(2,1)S(1)} fusion(pred[2]{0:T(512)(128)(4,1)S(1)} %iota_compare_fusion, bf16[128,1024]{1,0:T(8,128)(2,1)} %bitcast.22, bf16[128,1024]{1,0:T(8,128)(2,1)} %bitcast.23), kind=kLoop, calls=%fused_computation | loop fusion | flops 262144 | bytes 1048578 | tf_op jit(solution)/shard_map/jit(_where)/select_n | solution.py:209
  1.2 3.2 %collective-permute-start.2 = (bf16[2,128,1024]{2,1,0:T(8,128)(2,1)S(1)}, bf16[2,128,1024]{2,1,0:T(8,128)(2,1)S(1)}, u32[]{:S(2)}, u32[]{:S(2)}) collective-permute-start(bf16[2,128,1024]{2,1,0:T(8,128)(2,1)S(1)} %broadcast_select_fusion.refs_1_.refs_3_), channel_id=1, source_target_pairs={{0,4},{1,5},{2,6},{3,7},{4,8},{5,9},{6,10},{7,11},{8,12},{9,13},{1... | collective-permute-start | bytes 1572872 | tf_op jit(solution)/shard_map/ppermute | solution.py:244
  4.4 1.3 %collective-permute-start.1 = (bf16[2,128,1024]{2,1,0:T(8,128)(2,1)S(1)}, bf16[2,128,1024]{2,1,0:T(8,128)(2,1)S(1)}, u32[]{:S(2)}, u32[]{:S(2)}) collective-permute-start(bf16[2,128,1024]{2,1,0:T(8,128)(2,1)S(1)} %broadcast_select_fusion.refs_1_.refs_3_), channel_id=1, source_target_pairs={{0,1},{2,3},{4,5},{6,7},{8,9},{10,11},{12,13},{14,15},{16,17},{18,... | collective-permute-start | bytes 1572872 | tf_op jit(solution)/shard_map/ppermute | solution.py:244
  5.7 3.1 %collective-permute-start = (bf16[2,128,1024]{2,1,0:T(8,128)(2,1)S(1)}, bf16[2,128,1024]{2,1,0:T(8,128)(2,1)S(1)}, u32[]{:S(2)}, u32[]{:S(2)}) collective-permute-start(bf16[2,128,1024]{2,1,0:T(8,128)(2,1)S(1)} %broadcast_select_fusion.refs_1_.refs_3_), channel_id=1, source_target_pairs={{0,2},{1,3},{4,6},{5,7},{8,10},{9,11},{12,14},{13,15},{16,18},{17,... | collective-permute-start | bytes 1572872 | tf_op jit(solution)/shard_map/ppermute | solution.py:244
  8.8 7.0 %collective-permute-done.2.refs_3_.refs_5_ = bf16[2,128,1024]{2,1,0:T(8,128)(2,1)S(1)} collective-permute-done((bf16[2,128,1024]{2,1,0:T(8,128)(2,1)S(1)}, bf16[2,128,1024]{2,1,0:T(8,128)(2,1)S(1)}, u32[]{:S(2)}, u32[]{:S(2)}) %collective-permute-start.2) | collective-permute-done | bytes 524320 | tf_op jit(solution)/shard_map/ppermute | solution.py:244
  15.8 3.2 %collective-permute-start.4 = (bf16[2,128,1024]{2,1,0:T(8,128)(2,1)S(1)}, bf16[2,128,1024]{2,1,0:T(8,128)(2,1)S(1)}, u32[]{:S(2)}, u32[]{:S(2)}) collective-permute-start(bf16[2,128,1024]{2,1,0:T(8,128)(2,1)S(1)} %collective-permute-done.2.refs_3_.refs_5_), channel_id=1, source_target_pairs={{4,8},{5,9},{6,10},{7,11},{8,12},{9,13},{10,14},{11,15},{20,24},{2... | collective-permute-start | bytes 1572872 | tf_op jit(solution)/shard_map/ppermute | solution.py:244
  19.0 3.1 %collective-permute-start.3 = (bf16[2,128,1024]{2,1,0:T(8,128)(2,1)S(1)}, bf16[2,128,1024]{2,1,0:T(8,128)(2,1)S(1)}, u32[]{:S(2)}, u32[]{:S(2)}) collective-permute-start(bf16[2,128,1024]{2,1,0:T(8,128)(2,1)S(1)} %collective-permute-done.2.refs_3_.refs_5_), channel_id=1, source_target_pairs={{6,4},{7,5},{4,6},{5,7},{10,8},{11,9},{8,10},{9,11},{14,12},{15,13... | collective-permute-start | bytes 1572872 | tf_op jit(solution)/shard_map/ppermute | solution.py:244
  22.4 0.7 concatenate.3.info
  23.1 0.0 collective-permute-done.1.refs_2_.refs_4_
  23.1 0.0 collective-permute-done.refs_4_.refs_6_
  23.1 4.0 %collective-permute-start.6 = (bf16[2,128,1024]{2,1,0:T(8,128)(2,1)S(1)}, bf16[2,128,1024]{2,1,0:T(8,128)(2,1)S(1)}, u32[]{:S(2)}, u32[]{:S(2)}) collective-permute-start(bf16[2,128,1024]{2,1,0:T(8,128)(2,1)S(1)} %collective-permute-done.2.refs_3_.refs_5_), channel_id=1, source_target_pairs={{5,4},{4,5},{7,6},{6,7},{9,8},{8,9},{11,10},{10,11},{13,12},{12,13... | collective-permute-start | bytes 1572872 | tf_op jit(solution)/shard_map/ppermute | solution.py:244
  27.1 0.0 copy-start
  27.2 1.6 %copy-done = bf16[1,128,8192]{2,1,0:T(8,128)(2,1)S(1)} copy-done((bf16[1,128,8192]{2,1,0:T(8,128)(2,1)S(1)}, bf16[1,128,8192]{2,1,0:T(8,128)(2,1)}, u32[]{:S(2)}) %copy-start) | copy-done | bytes 2097176
  28.7 5.4 %shard_map.46 = (f32[128,8192]{1,0:T(8,128)S(1)}, f32[8,128,128]{2,1,0:T(8,128)S(1)}) custom-call(s32[22]{0:T(128)S(1)} %concatenate.3.info, bf16[128,8192]{1,0:T(8,128)(2,1)S(1)} %bitcast.19, bf16[2,128,1024]{2,1,0:T(8,128)(2,1)S(1)} %broadcast_select_fusion.refs_1_.refs_3_, bf16[2,128,1024]{2,1,0:T(8,128)(2,1)S(1)} %collective-permute-done.1.refs_2_.refs_4_, ...), custom_call_target="tpu_custom_call" | custom-call | flops 16777216 | bytes 1048576 | tf_op jit(solution)/shard_map/pallas_call | solution.py:195
  34.2 0.0 collective-permute-done.4.refs_4_.refs_8_
  34.2 0.1 broadcast_select_fusion.1
  34.3 1.9 %collective-permute-start.5 = (bf16[2,128,1024]{2,1,0:T(8,128)(2,1)S(1)}, bf16[2,128,1024]{2,1,0:T(8,128)(2,1)S(1)}, u32[]{:S(2)}, u32[]{:S(2)}) collective-permute-start(bf16[2,128,1024]{2,1,0:T(8,128)(2,1)S(1)} %broadcast_select_fusion.1), channel_id=1, source_target_pairs={{10,8},{14,12},{5,9},{9,13},{26,24},{30,28},{21,25},{25,29}} | collective-permute-start | bytes 1572872 | tf_op jit(solution)/shard_map/ppermute | solution.py:244
  36.2 2.4 %collective-permute-start.7 = (bf16[2,128,1024]{2,1,0:T(8,128)(2,1)S(1)}, bf16[2,128,1024]{2,1,0:T(8,128)(2,1)S(1)}, u32[]{:S(2)}, u32[]{:S(2)}) collective-permute-start(bf16[2,128,1024]{2,1,0:T(8,128)(2,1)S(1)} %collective-permute-done.4.refs_4_.refs_8_), channel_id=1, source_target_pairs={{9,8},{8,9},{11,10},{10,11},{13,12},{12,13},{15,14},{14,15},{25,24... | collective-permute-start | bytes 1572872 | tf_op jit(solution)/shard_map/ppermute | solution.py:244
  38.6 2.0 %collective-permute-start.9 = (bf16[2,128,1024]{2,1,0:T(8,128)(2,1)S(1)}, bf16[2,128,1024]{2,1,0:T(8,128)(2,1)S(1)}, u32[]{:S(2)}, u32[]{:S(2)}) collective-permute-start(bf16[2,128,1024]{2,1,0:T(8,128)(2,1)S(1)} %collective-permute-done.3.refs_5_.refs_9_), channel_id=1, source_target_pairs={{5,4},{4,5},{7,6},{6,7},{9,8},{8,9},{11,10},{10,11},{13,12},{12,13... | collective-permute-start | bytes 1572872 | tf_op jit(solution)/shard_map/ppermute | solution.py:244
  40.5 0.7 collective-permute-start.8
  41.2 5.6 %shard_map.47 = (f32[128,8192]{1,0:T(8,128)S(1)}, f32[8,128,128]{2,1,0:T(8,128)S(1)}) custom-call(s32[22]{0:T(128)S(1)} %concatenate.3.info, bf16[128,8192]{1,0:T(8,128)(2,1)S(1)} %bitcast.20, f32[128,8192]{1,0:T(8,128)S(1)} %get-tuple-element.25.refs_1_, f32[8,128,128]{2,1,0:T(8,128)S(1)} %get-tuple-element.26.refs_2_, ...), custom_call_target="tpu_custom_call" | custom-call | flops 16777216 | bytes 1048576 | tf_op jit(solution)/shard_map/pallas_call | solution.py:195
  46.8 2.4 %collective-permute-start.10 = (bf16[2,128,1024]{2,1,0:T(8,128)(2,1)S(1)}, bf16[2,128,1024]{2,1,0:T(8,128)(2,1)S(1)}, u32[]{:S(2)}, u32[]{:S(2)}) collective-permute-start(bf16[2,128,1024]{2,1,0:T(8,128)(2,1)S(1)} %collective-permute-done.5.refs_13_), channel_id=1, source_target_pairs={{9,8},{8,9},{13,12},{12,13},{25,24},{24,25},{29,28},{28,29}} | collective-permute-start | bytes 1572872 | tf_op jit(solution)/shard_map/ppermute | solution.py:244
  49.2 1.5 %collective-permute-done.10.refs_14_ = bf16[2,128,1024]{2,1,0:T(8,128)(2,1)S(1)} collective-permute-done((bf16[2,128,1024]{2,1,0:T(8,128)(2,1)S(1)}, bf16[2,128,1024]{2,1,0:T(8,128)(2,1)S(1)}, u32[]{:S(2)}, u32[]{:S(2)}) %collective-permute-start.10) | collective-permute-done | bytes 524320 | tf_op jit(solution)/shard_map/ppermute | solution.py:244
  50.7 52.0 %shard_map.48 = bf16[128,8192]{1,0:T(8,128)(2,1)} custom-call(s32[22]{0:T(128)S(1)} %concatenate.3.info, bf16[128,8192]{1,0:T(8,128)(2,1)S(1)} %bitcast.21, f32[128,8192]{1,0:T(8,128)S(1)} %get-tuple-element.29.refs_1_, f32[8,128,128]{2,1,0:T(8,128)S(1)} %get-tuple-element.30.refs_2_, bf16[2,128,1024]{2,1,0:T(8,128)(2,1)S(1)} %broadcast_select_fusion.refs_1_.refs_3_, ...), custom_call_target="tpu_custom_call" | custom-call | flops 16777216 | bytes 1048576 | tf_op jit(solution)/shard_map/pallas_call | solution.py:195
  (7 shorter events, 0.0 us)
Async XLA Ops:
  1.2 14.7 %collective-permute-start.2 = (bf16[2,128,1024]{2,1,0:T(8,128)(2,1)S(1)}, bf16[2,128,1024]{2,1,0:T(8,128)(2,1)S(1)}, u32[]{:S(2)}, u32[]{:S(2)}) collective-permute-start(bf16[2,128,1024]{2,1,0:T(8,128)(2,1)S(1)} %broadcast_select_fusion.refs_1_.refs_3_), channel_id=1, source_target_pairs={{0,4},{1,5},{2,6},{3,7},{4,8},{5,9},{6,10},{7,11},{8,12},{9,13},{1... | collective-permute-start | bytes 1572872 | tf_op jit(solution)/shard_map/ppermute | solution.py:244
  4.4 18.7 %collective-permute-start.1 = (bf16[2,128,1024]{2,1,0:T(8,128)(2,1)S(1)}, bf16[2,128,1024]{2,1,0:T(8,128)(2,1)S(1)}, u32[]{:S(2)}, u32[]{:S(2)}) collective-permute-start(bf16[2,128,1024]{2,1,0:T(8,128)(2,1)S(1)} %broadcast_select_fusion.refs_1_.refs_3_), channel_id=1, source_target_pairs={{0,1},{2,3},{4,5},{6,7},{8,9},{10,11},{12,13},{14,15},{16,17},{18,... | collective-permute-start | bytes 1572872 | tf_op jit(solution)/shard_map/ppermute | solution.py:244
  5.7 17.4 %collective-permute-start = (bf16[2,128,1024]{2,1,0:T(8,128)(2,1)S(1)}, bf16[2,128,1024]{2,1,0:T(8,128)(2,1)S(1)}, u32[]{:S(2)}, u32[]{:S(2)}) collective-permute-start(bf16[2,128,1024]{2,1,0:T(8,128)(2,1)S(1)} %broadcast_select_fusion.refs_1_.refs_3_), channel_id=1, source_target_pairs={{0,2},{1,3},{4,6},{5,7},{8,10},{9,11},{12,14},{13,15},{16,18},{17,... | collective-permute-start | bytes 1572872 | tf_op jit(solution)/shard_map/ppermute | solution.py:244
  15.8 18.3 %collective-permute-start.4 = (bf16[2,128,1024]{2,1,0:T(8,128)(2,1)S(1)}, bf16[2,128,1024]{2,1,0:T(8,128)(2,1)S(1)}, u32[]{:S(2)}, u32[]{:S(2)}) collective-permute-start(bf16[2,128,1024]{2,1,0:T(8,128)(2,1)S(1)} %collective-permute-done.2.refs_3_.refs_5_), channel_id=1, source_target_pairs={{4,8},{5,9},{6,10},{7,11},{8,12},{9,13},{10,14},{11,15},{20,24},{2... | collective-permute-start | bytes 1572872 | tf_op jit(solution)/shard_map/ppermute | solution.py:244
  19.0 15.1 %collective-permute-start.3 = (bf16[2,128,1024]{2,1,0:T(8,128)(2,1)S(1)}, bf16[2,128,1024]{2,1,0:T(8,128)(2,1)S(1)}, u32[]{:S(2)}, u32[]{:S(2)}) collective-permute-start(bf16[2,128,1024]{2,1,0:T(8,128)(2,1)S(1)} %collective-permute-done.2.refs_3_.refs_5_), channel_id=1, source_target_pairs={{6,4},{7,5},{4,6},{5,7},{10,8},{11,9},{8,10},{9,11},{14,12},{15,13... | collective-permute-start | bytes 1572872 | tf_op jit(solution)/shard_map/ppermute | solution.py:244
  23.1 18.1 %collective-permute-start.6 = (bf16[2,128,1024]{2,1,0:T(8,128)(2,1)S(1)}, bf16[2,128,1024]{2,1,0:T(8,128)(2,1)S(1)}, u32[]{:S(2)}, u32[]{:S(2)}) collective-permute-start(bf16[2,128,1024]{2,1,0:T(8,128)(2,1)S(1)} %collective-permute-done.2.refs_3_.refs_5_), channel_id=1, source_target_pairs={{5,4},{4,5},{7,6},{6,7},{9,8},{8,9},{11,10},{10,11},{13,12},{12,13... | collective-permute-start | bytes 1572872 | tf_op jit(solution)/shard_map/ppermute | solution.py:244
  27.1 1.6 %copy-start = (bf16[1,128,8192]{2,1,0:T(8,128)(2,1)S(1)}, bf16[1,128,8192]{2,1,0:T(8,128)(2,1)}, u32[]{:S(2)}) copy-start(bf16[1,128,8192]{2,1,0:T(8,128)(2,1)} %param.4) | copy-start | bytes 6291460
  34.3 12.6 %collective-permute-start.5 = (bf16[2,128,1024]{2,1,0:T(8,128)(2,1)S(1)}, bf16[2,128,1024]{2,1,0:T(8,128)(2,1)S(1)}, u32[]{:S(2)}, u32[]{:S(2)}) collective-permute-start(bf16[2,128,1024]{2,1,0:T(8,128)(2,1)S(1)} %broadcast_select_fusion.1), channel_id=1, source_target_pairs={{10,8},{14,12},{5,9},{9,13},{26,24},{30,28},{21,25},{25,29}} | collective-permute-start | bytes 1572872 | tf_op jit(solution)/shard_map/ppermute | solution.py:244
  36.2 13.0 %collective-permute-start.7 = (bf16[2,128,1024]{2,1,0:T(8,128)(2,1)S(1)}, bf16[2,128,1024]{2,1,0:T(8,128)(2,1)S(1)}, u32[]{:S(2)}, u32[]{:S(2)}) collective-permute-start(bf16[2,128,1024]{2,1,0:T(8,128)(2,1)S(1)} %collective-permute-done.4.refs_4_.refs_8_), channel_id=1, source_target_pairs={{9,8},{8,9},{11,10},{10,11},{13,12},{12,13},{15,14},{14,15},{25,24... | collective-permute-start | bytes 1572872 | tf_op jit(solution)/shard_map/ppermute | solution.py:244
  38.6 10.7 %collective-permute-start.9 = (bf16[2,128,1024]{2,1,0:T(8,128)(2,1)S(1)}, bf16[2,128,1024]{2,1,0:T(8,128)(2,1)S(1)}, u32[]{:S(2)}, u32[]{:S(2)}) collective-permute-start(bf16[2,128,1024]{2,1,0:T(8,128)(2,1)S(1)} %collective-permute-done.3.refs_5_.refs_9_), channel_id=1, source_target_pairs={{5,4},{4,5},{7,6},{6,7},{9,8},{8,9},{11,10},{10,11},{13,12},{12,13... | collective-permute-start | bytes 1572872 | tf_op jit(solution)/shard_map/ppermute | solution.py:244
  40.5 8.7 %collective-permute-start.8 = (bf16[2,128,1024]{2,1,0:T(8,128)(2,1)S(1)}, bf16[2,128,1024]{2,1,0:T(8,128)(2,1)S(1)}, u32[]{:S(2)}, u32[]{:S(2)}) collective-permute-start(bf16[2,128,1024]{2,1,0:T(8,128)(2,1)S(1)} %collective-permute-done.refs_4_.refs_6_), channel_id=1, source_target_pairs={{3,2},{2,3},{7,6},{6,7},{11,10},{10,11},{15,14},{14,15},{19,18},{1... | collective-permute-start | bytes 1572872 | tf_op jit(solution)/shard_map/ppermute | solution.py:244
  46.8 3.9 %collective-permute-start.10 = (bf16[2,128,1024]{2,1,0:T(8,128)(2,1)S(1)}, bf16[2,128,1024]{2,1,0:T(8,128)(2,1)S(1)}, u32[]{:S(2)}, u32[]{:S(2)}) collective-permute-start(bf16[2,128,1024]{2,1,0:T(8,128)(2,1)S(1)} %collective-permute-done.5.refs_13_), channel_id=1, source_target_pairs={{9,8},{8,9},{13,12},{12,13},{25,24},{24,25},{29,28},{28,29}} | collective-permute-start | bytes 1572872 | tf_op jit(solution)/shard_map/ppermute | solution.py:244
